TPU v7x, 128 devices: a whole 4x4x4 slice. The times are simulated.
128 devices in a mesh: seq: 8 (over y_hi, z), res: 16 (over y_lo, x, core).
Axes of the slice: x: 4, y: 4 (y_hi: 2, y_lo: 2; y = y_hi * 2 + y_lo), z: 4, core: 2. Of those that a mesh axis runs over, the one named last changes fastest.
Arguments:
- homology_table: bfloat16 [64, 2560, 256], P('seq', 'res'), may hold values from -6 to 6
- coupled_state: bfloat16 [2560, 2560, 128], P('seq', 'res'), may hold values from -6 to 6
- aligned_indicator: int32 [64, 2560], P('seq', 'res'), may hold values 0 or 1
- amino_indicator: int32 [2560], P('res'), may hold values 0 or 1
- horizontal_scaling_factor: float32 [256], replicated, may hold values from 0.25 to 1.75
- horizontal_projection_matrix: bfloat16 [256, 1024], replicated, may hold values from -6 to 6
- horizontal_sigmoid_shift: float32 [256], replicated, may hold values from -6 to 6
- horizontal_result_matrix: bfloat16 [256, 256], replicated, may hold values from -0.375 to 0.375
- horizontal_result_shift: float32 [256], replicated, may hold values from -3 to 3
- coupling_scaling_factor: float32 [128], replicated, may hold values from 0.25 to 1.75
- coupling_head_matrix: bfloat16 [128, 8], replicated, may hold values from -2 to 2
- downward_stretch_vector: float32 [256], replicated, may hold values from 0.25 to 1.75
- vertical_projection_matrix: bfloat16 [256, 1024], replicated, may hold values from -6 to 6
- vertical_sigmoid_shift: float32 [256], replicated, may hold values from -6 to 6
- vertical_result_matrix: bfloat16 [256, 256], replicated, may hold values from -0.375 to 0.375
- vertical_result_shift: float32 [256], replicated, may hold values from -3 to 3
- feedforward_scaling_factor: float32 [256], replicated, may hold values from 0.25 to 1.75
- feedforward_expand_matrix: bfloat16 [256, 1024], replicated, may hold values from -0.375 to 0.375
- feedforward_shrink_matrix: bfloat16 [1024, 256], replicated, may hold values from -0.1875 to 0.1875
Outputs:
- updated: bfloat16 [64, 2560, 256], P('seq', 'res')
All inputs are finite; a program needn't handle non-finite values. No bound on the sum of `aligned_indicator` or of `amino_indicator` on one device may be relied on, other than what follows from the above.
Results may differ from a plain program's by a relative error of at most 0.025.
Values may be sent and summed in bfloat16 or wider, within the bound.
No kernel may reach another device: no remote copies, remote signals or barrier semaphores. Data moves between devices by JAX's collectives and lax.ppermute only.
A program may use at most 256 MiB of HBM per device.

v0:
```python
import functools
import math

import jax
import jax.numpy as jnp
from jax import lax
from jax.experimental import pallas as pl
from jax.experimental.pallas import tpu as pltpu
from jax.sharding import PartitionSpec as P

F32 = jnp.float32
BF16 = jnp.bfloat16
EPS = 1e-05
LOG2E = 1.4426950408889634
LANES = 128
MASKED = -1e30
VMEM = 56 * 2**20
ROW_VMEM = 40 * 2**20


def dot(a, b):
    return jnp.dot(a, b, preferred_element_type=F32)


def dot_nt(a, b):
    return lax.dot_general(a, b, (((1,), (1,)), ((), ())), preferred_element_type=F32)


def dot_tn(a, b):
    return lax.dot_general(a, b, (((0,), (0,)), ((), ())), preferred_element_type=F32)


def normalize(values, gain):
    center = values - jnp.mean(values, axis=-1, keepdims=True)
    spread = jnp.mean(center * center, axis=-1, keepdims=True)
    return center * lax.rsqrt(spread + EPS) * gain


def lanes_of(shape):
    return lax.broadcasted_iota(jnp.int32, shape, len(shape) - 1)


STEP = 32
GROUPS = 4
EIGHT = 8
STEP_ROWS = STEP + EIGHT


def pair_kernel(pair_ref, gain_ref, head_ref, bias_ref, project_ref, rows_ref):
    channels, heads = head_ref.shape

    @pl.when(pl.program_id(0) == 0)
    def _():
        gained = (gain_ref[...] * LOG2E) * head_ref[...].astype(F32).T
        gained = gained - jnp.mean(gained, axis=1, keepdims=True)
        high = gained.astype(BF16)
        low = (gained - high.astype(F32)).astype(BF16)
        same = lax.broadcasted_iota(jnp.int32, (channels, channels), 0) == lanes_of((channels, channels))
        centering = jnp.where(same, 1.0, 0.0) - 1.0 / channels
        project_ref[:channels] = centering.astype(BF16)
        project_ref[channels:] = jnp.concatenate([high.astype(F32), low.astype(F32)], axis=0).astype(BF16)

    def project(tokens):
        both = dot_nt(project_ref[...], tokens)
        center = both[:channels]
        spread = jnp.sum(center * center, axis=0, keepdims=True) * (1.0 / channels)
        raw = both[channels : channels + heads] + both[channels + heads :]
        return raw * lax.rsqrt(spread + EPS)

    for i in range(0, STEP, 2):
        done = project(pair_ref[i : i + 2, :LANES, :].reshape(2 * LANES, channels))
        rows_ref[:, i, :] = done[:, :LANES]
        rows_ref[:, i + 1, :] = done[:, LANES:]
    for r in range(0, EIGHT, 2):
        rest = [pair_ref[g * EIGHT + r + e, LANES:, :] for e in range(2) for g in range(GROUPS)]
        done = project(jnp.concatenate(rest, axis=0))
        rows_ref[:, STEP + r, :] = done[:, :LANES]
        rows_ref[:, STEP + r + 1, :] = done[:, LANES:]
    bias_ref[:, 0] = rows_ref[...].astype(BF16)


def pair_bias(coupled, gain, head_matrix):
    rows, cols, channels = coupled.shape
    heads = head_matrix.shape[1]
    return pl.pallas_call(
        pair_kernel,
        grid=(rows // STEP,),
        in_specs=[
            pl.BlockSpec((STEP, cols, channels), lambda i: (i, 0, 0)),
            pl.BlockSpec((1, channels), lambda i: (0, 0)),
            pl.BlockSpec((channels, heads), lambda i: (0, 0)),
        ],
        out_specs=pl.BlockSpec((heads, 1, STEP_ROWS, LANES), lambda i: (0, i, 0, 0)),
        out_shape=jax.ShapeDtypeStruct((heads, rows // STEP, STEP_ROWS, LANES), BF16),
        scratch_shapes=[
            pltpu.VMEM((channels + 2 * heads, channels), BF16),
            pltpu.VMEM((heads, STEP_ROWS, LANES), F32),
        ],
        compiler_params=pltpu.CompilerParams(vmem_limit_bytes=VMEM),
        name="pair_bias",
    )(coupled, gain[None], head_matrix)


MASK_ROWS = 16


def pack_kernel(table_ref, mask_ref, gain_ref, weight_ref, packed_ref, *, scale):
    group, residues, channels = table_ref.shape
    heads = packed_ref.shape[0]
    head_size = channels // heads
    lane = lanes_of((residues, LANES))
    flat = []
    for member in range(group):
        normed = normalize(table_ref[member].astype(F32), gain_ref[...]).astype(BF16)
        flat.append(dot(normed, weight_ref[:, : 3 * channels]))
    for h in range(heads):
        for kind in range(3):
            column = kind * channels + h // group * LANES
            total = None
            for member in range(group):
                part = flat[member][:, column : column + LANES]
                if member != h % group:
                    part = pltpu.roll(part, ((member - h % group) * head_size) % LANES, 1)
                total = part if total is None else jnp.where(lane >= member * head_size, part, total)
            if kind == 0:
                total = total * scale
            packed_ref[h, 0, kind * residues : (kind + 1) * residues] = total.astype(BF16)
        packed_ref[h, 0, 3 * residues :] = mask_ref[0]


def pack_heads(table, mask, gain, weight, heads, scale):
    lines, residues, channels = table.shape
    group = LANES * heads // channels
    packs = lines // group
    rows = 3 * residues + MASK_ROWS
    mask = jnp.pad(mask, ((0, MASK_ROWS - lines), (0, packs * LANES - residues)))
    mask = jnp.transpose(mask.reshape(MASK_ROWS, packs, LANES), (1, 0, 2)).astype(BF16)
    return pl.pallas_call(
        functools.partial(pack_kernel, scale=scale),
        grid=(packs,),
        in_specs=[
            pl.BlockSpec((group, residues, channels), lambda s: (s, 0, 0)),
            pl.BlockSpec((1, MASK_ROWS, LANES), lambda s: (s, 0, 0)),
            pl.BlockSpec((1, channels), lambda s: (0, 0)),
            pl.BlockSpec(weight.shape, lambda s: (0, 0)),
        ],
        out_specs=pl.BlockSpec((heads, 1, rows, LANES), lambda s: (0, s, 0, 0)),
        out_shape=jax.ShapeDtypeStruct((heads, packs, rows, LANES), BF16),
        compiler_params=pltpu.CompilerParams(vmem_limit_bytes=VMEM),
        name="pack_heads",
    )(table, mask, gain[None, :], weight)


TILE = 16


def row_kernel(place_ref, own_ref, other_ref, *rest, turn, count, residues, head_size):
    bias_refs, rest = rest[:count], rest[count:]
    out_ref, bias32_ref, key_ref, value_ref, score_ref, weight_ref = rest[-6:]
    earlier = rest[:-6]
    blocks, packs, _, _ = own_ref.shape
    lines, keys, _ = key_ref.shape
    pieces, targets = out_ref.shape[:2]
    span = residues // pieces
    group = LANES // head_size
    chunk = 2 * LANES
    main = 2 * blocks * LANES
    core = place_ref[0]
    there = (place_ref[1] + turn) % 2 * count
    lane8 = lanes_of((EIGHT, LANES))
    lane = lanes_of((residues, LANES))

    for ref in earlier:
        for z in range(ref.shape[1]):
            out_ref[:, place_ref[1] * count + z] = ref[:, z]

    def gather_tails(tails, at):
        total = None
        for e, moved in enumerate(tails):
            if e != at:
                moved = pltpu.roll(moved, ((e - at) * STEP) % LANES, 1)
            total = moved if total is None else jnp.where(lane8 >= e * STEP, moved, total)
        return total

    for block, ref in enumerate(bias_refs):
        for side in range(2):
            parity = core if side == 0 else 1 - core
            for step in range(residues // STEP):
                row = step * STEP
                tails = []
                for k in range(blocks):
                    tile = ref[2 * k + parity, step].astype(F32)
                    column = (side * blocks + k) * LANES
                    bias32_ref[block, row : row + STEP, column : column + LANES] = tile[:STEP]
                    tails.append(tile[STEP:])
                for q in range(blocks // GROUPS):
                    column = main + (side * blocks // GROUPS + q) * LANES
                    for g in range(GROUPS):
                        bias32_ref[block, row + g * EIGHT : row + (g + 1) * EIGHT, column : column + LANES] = (
                            gather_tails(tails[q * GROUPS : (q + 1) * GROUPS], g)
                        )

    def upright(rows):
        wide = jnp.concatenate([rows, jnp.zeros((head_size - lines, LANES), F32)] * group, axis=0)
        return wide.T.astype(BF16)

    lane1 = lanes_of((1, LANES)) // head_size
    for side, ref in enumerate((own_ref, other_ref)):
        for q in range(blocks // GROUPS):
            masks = [ref[q * GROUPS + e, :, 3 * residues :, :].astype(F32) for e in range(GROUPS)]
            rest_mask = upright(gather_tails([m[1, :lines] for m in masks], 0))
            for e in range(GROUPS):
                k = q * GROUPS + e
                first_mask = upright(masks[e][0, :lines])
                head_at = (side * blocks + k) * LANES
                tail_at = main + (side * blocks + k) * STEP
                for pack in range(packs):
                    key = ref[k, pack, residues : 2 * residues, :]
                    value = ref[k, pack, 2 * residues : 3 * residues, :]
                    for member in range(group):
                        s = pack * group + member
                        spare = jnp.where(lane1 == (member + 1) % group, 1.0, 0.0)
                        keep, spare = (1.0 - spare).astype(BF16), spare.astype(BF16)
                        kept = key * keep
                        key_ref[s, head_at : head_at + LANES] = kept[:LANES] + first_mask * spare
                        key_ref[s, tail_at : tail_at + STEP] = (
                            kept[LANES:] + rest_mask[e * STEP : (e + 1) * STEP] * spare
                        )
                        kept = value * keep + spare
                        value_ref[s, head_at : head_at + LANES] = kept[:LANES]
                        value_ref[s, tail_at : tail_at + STEP] = kept[LANES:]

    def body(block, carry):
        ahead = jnp.where(block == 1, -1, jnp.where(block == 2, 1, jnp.where(block == 3, 2, 0)))
        place = there + (place_ref[2] + ahead + count) % count

        def query_of(s):
            member = s % group
            spare = (member + 1) % group * head_size + s
            inside = (lane >= member * head_size) & (lane < (member + 1) * head_size)
            raw = own_ref[place, s // group, :residues, :].astype(F32)
            return jnp.where(inside, raw, jnp.where(lane == spare, 1.0, 0.0)).astype(BF16)

        def score(s, query, j):
            columns = slice(j * chunk, (j + 1) * chunk)
            score_ref[s % 2, :, columns] = dot_nt(query, key_ref[s, columns, :]) + bias32_ref[block, :, columns]

        def weigh(s, row):
            scores = score_ref[s % 2, row : row + TILE, :]
            top = jnp.max(scores, axis=1, keepdims=True)
            weight_ref[s % 2, row : row + TILE, :] = jnp.exp2(scores - top).astype(BF16)

        query = query_of(0)
        for j in range(keys // chunk):
            score(0, query, j)
        total = None
        for s in range(lines):
            member, pack = s % group, s // group
            query = query_of(s + 1) if s + 1 < lines else None
            steps = keys // chunk
            tiles = residues // TILE
            for j in range(steps):
                if query is not None:
                    score(s + 1, query, j)
                for r in range(j * tiles // steps, (j + 1) * tiles // steps):
                    weigh(s, r * TILE)
            mixed = dot(weight_ref[s % 2], value_ref[s])
            spare = (member + 1) % group * head_size
            mixed = mixed / mixed[:, spare : spare + 1]
            total = mixed if member == 0 else jnp.where(lane >= member * head_size, mixed, total)
            if member == group - 1:
                for piece in range(pieces):
                    part = total[piece * span : (piece + 1) * span].astype(BF16)
                    out_ref[piece, place % targets, pack * span : (pack + 1) * span, :] = part
        return carry

    lax.fori_loop(0, count, body, 0)


def row_attention(place, own, other, biases, earlier, turn, residues, pieces, head_size):
    blocks, packs, _, _ = own.shape
    lines = packs * LANES // head_size
    keys = 2 * blocks * residues
    count = len(biases)
    targets = count + sum(e.shape[1] for e in earlier)
    rows = packs * residues // pieces
    scores = lines * count * residues * keys
    return pl.pallas_call(
        functools.partial(row_kernel, turn=turn, count=count, residues=residues, head_size=head_size),
        in_specs=[pl.BlockSpec(memory_space=pltpu.SMEM)]
        + [pl.BlockSpec(memory_space=pltpu.VMEM)] * (2 + count + len(earlier)),
        out_specs=pl.BlockSpec(memory_space=pltpu.VMEM),
        out_shape=jax.ShapeDtypeStruct((pieces, targets, rows, LANES), BF16),
        scratch_shapes=[
            pltpu.VMEM((count, residues, keys), F32),
            pltpu.VMEM((lines, keys, LANES), BF16),
            pltpu.VMEM((lines, keys, LANES), BF16),
            pltpu.VMEM((2, residues, keys), F32),
            pltpu.VMEM((2, residues, keys), BF16),
        ],
        compiler_params=pltpu.CompilerParams(vmem_limit_bytes=ROW_VMEM),
        cost_estimate=pl.CostEstimate(flops=scores * 512, bytes_accessed=12_000_000, transcendentals=scores),
        name="row_attention",
    )(place, own, other, *biases, *earlier)


def column_kernel(
    mixed_ref, table_ref, mask_ref,
    row_gain_ref, row_gate_ref, row_shift_ref, row_out_ref, row_bias_ref,
    col_gain_ref, col_weight_ref, col_shift_ref, col_out_ref, col_bias_ref,
    ff_gain_ref, expand_ref, shrink_ref, out_ref, mixed32_ref, *, heads, scale,
):
    groups, span, lines, channels = table_ref.shape
    rows = groups * lines
    head_size = channels // heads

    @pl.when(pl.program_id(0) == 0)
    def _():
        members = LANES // head_size
        packs = lines // members
        received = mixed_ref.shape[2]
        residues = received // packs
        source = lax.broadcasted_iota(jnp.int32, (LANES, channels), 0)
        target = lanes_of((LANES, channels))
        tokens = [mixed_ref[:, h].astype(F32).reshape(groups * received, LANES).astype(BF16) for h in range(heads)]
        for member in range(members):
            total = None
            for h in range(heads):
                move = (target // head_size == h) & (source == target - h * head_size + member * head_size)
                part = dot(tokens[h], jnp.where(move, 1.0, 0.0).astype(BF16))
                total = part if total is None else total + part
            for r in range(groups):
                for pack in range(packs):
                    row = r * received + pack * residues
                    line = r * lines + pack * members + member
                    for part in range(channels // LANES):
                        mixed32_ref[part, pl.ds(line, residues, stride=rows), :] = total[
                            row : row + residues, part * LANES : (part + 1) * LANES
                        ]

    table = table_ref[...].astype(F32)
    table = jnp.concatenate([table[:, i].reshape(rows, channels) for i in range(span)], axis=0)
    here = pl.ds(pl.program_id(0) * span * rows, span * rows)
    mixed = jnp.concatenate([mixed32_ref[part, here, :] for part in range(channels // LANES)], axis=1)

    row_in = normalize(table, row_gain_ref[...]).astype(BF16)
    gate = jax.nn.sigmoid(dot(row_in, row_gate_ref[...]) + row_shift_ref[...])
    gated = (mixed * gate).astype(BF16)
    after_rows = table + (dot(gated, row_out_ref[...]) + row_bias_ref[...])
    after_rows = after_rows.astype(BF16).astype(F32)

    col_in = normalize(after_rows, col_gain_ref[...]).astype(BF16)
    projected = dot(col_in, col_weight_ref[...])
    query = (projected[:, :channels] * scale).astype(BF16)
    key = projected[:, channels : 2 * channels].astype(BF16)
    value = projected[:, 2 * channels : 3 * channels].astype(BF16)
    gate = jax.nn.sigmoid(projected[:, 3 * channels :] + col_shift_ref[...])

    shape = (heads * rows, channels)
    row_head = lax.broadcasted_iota(jnp.int32, shape, 0) // rows
    same = row_head == lax.broadcasted_iota(jnp.int32, shape, 1) // head_size
    same = jnp.where(same, 1.0, 0.0).astype(BF16)
    masks = mask_ref[:, 0].astype(F32).reshape(rows, channels)
    mask_lane = lanes_of((rows, channels))
    attended = []
    for i in range(span):
        here = slice(i * rows, (i + 1) * rows)
        spread_key = jnp.concatenate([key[here]] * heads, axis=0) * same
        spread_value = jnp.concatenate([value[here]] * heads, axis=0) * same
        scores = dot_nt(spread_key, query[here]).reshape(heads, rows, rows)
        place = pl.program_id(0) * span + i
        present = jnp.sum(jnp.where(mask_lane == place, masks, 0.0), axis=1, keepdims=True)
        scores = jnp.where(present[None] > 0, scores, -1e9)
        top = jnp.max(scores, axis=1, keepdims=True)
        weights = jnp.exp2(scores - top)
        weights = weights / jnp.sum(weights, axis=1, keepdims=True)
        weights = weights.astype(BF16).reshape(heads * rows, rows)
        attended.append(dot_tn(weights, spread_value))
    gated = (jnp.concatenate(attended, axis=0) * gate).astype(BF16)
    after_cols = after_rows + (dot(gated, col_out_ref[...]) + col_bias_ref[...])
    after_cols = after_cols.astype(BF16).astype(F32)

    trans_in = normalize(after_cols, ff_gain_ref[...]).astype(BF16)
    hidden = jnp.maximum(dot(trans_in, expand_ref[...]), 0.0).astype(BF16)
    updated = after_cols + dot(hidden, shrink_ref[...])
    for i in range(span):
        block = updated[i * rows : (i + 1) * rows].reshape(groups, lines, channels)
        out_ref[:, i] = block.astype(BF16)


def column_phase(mixed, table, params, heads, scale, span):
    groups, extended, lines, channels = table.shape
    residues = extended - 1
    token_block = pl.BlockSpec((groups, span, lines, channels), lambda i: (0, i, 0, 0))
    in_specs = [
        pl.BlockSpec(mixed.shape, lambda i: (0, 0, 0, 0)),
        token_block,
        pl.BlockSpec((groups, 1, lines, channels), lambda i: (0, residues, 0, 0)),
    ]
    in_specs += [pl.BlockSpec(p.shape, lambda i: (0, 0)) for p in params]
    return pl.pallas_call(
        functools.partial(column_kernel, heads=heads, scale=scale),
        grid=(residues // span,),
        in_specs=in_specs,
        out_specs=token_block,
        out_shape=jax.ShapeDtypeStruct((groups, residues, lines, channels), BF16),
        scratch_shapes=[pltpu.VMEM((channels // LANES, residues * groups * lines, LANES), F32)],
        compiler_params=pltpu.CompilerParams(vmem_limit_bytes=VMEM),
        name="column_phase",
    )(mixed, table, table, *params)


def shards(
    seq_size,
    res_size,
    homology_table,
    coupled_state,
    aligned_indicator,
    amino_indicator,
    horizontal_scaling_factor,
    horizontal_projection_matrix,
    horizontal_sigmoid_shift,
    horizontal_result_matrix,
    horizontal_result_shift,
    coupling_scaling_factor,
    coupling_head_matrix,
    downward_stretch_vector,
    vertical_projection_matrix,
    vertical_sigmoid_shift,
    vertical_result_matrix,
    vertical_result_shift,
    feedforward_scaling_factor,
    feedforward_expand_matrix,
    feedforward_shrink_matrix,
):
    lines, residues, channels = homology_table.shape
    heads = coupling_head_matrix.shape[1]
    head_size = channels // heads
    scale = LOG2E / math.sqrt(head_size)
    span = residues // seq_size
    core = lax.axis_index("res") % 2
    parity = [list(range(p, res_size, 2)) for p in (0, 1)]
    parity_all = [[r * res_size + c for r in range(seq_size) for c in group] for group in parity]

    tile_bias = pair_bias(coupled_state, coupling_scaling_factor, coupling_head_matrix)
    tile_bias, homology_table = lax.optimization_barrier((tile_bias, homology_table))
    steps = tile_bias.shape[1] // 2
    near = lax.all_to_all(tile_bias.reshape(res_size, steps, STEP_ROWS, LANES), "res", 0, 0)

    by_residue = jnp.transpose(homology_table, (1, 0, 2)).reshape(seq_size, span, lines, channels)
    mask_row = jnp.transpose(aligned_indicator.reshape(lines, seq_size, span), (1, 0, 2))
    mask_row = jnp.pad(mask_row.astype(BF16), ((0, 0), (0, 0), (0, channels - span)))
    columns = jnp.concatenate([by_residue, mask_row[:, None]], axis=1)

    present = aligned_indicator * amino_indicator[None, :]
    mask = jnp.where(present > 0, 0.0, MASKED).astype(F32)
    packed = pack_heads(
        homology_table, mask, horizontal_scaling_factor, horizontal_projection_matrix, heads, scale
    )
    me = lax.axis_index("seq")
    place = jnp.stack([core, me // (seq_size // 2), me % (seq_size // 2)]).astype(jnp.int32)
    near, packed, columns, place = lax.optimization_barrier((near, packed, columns, place))
    own = lax.all_to_all(packed, "res", 0, 0, axis_index_groups=parity)

    ring = seq_size // 2

    def around(values, by):
        return lax.ppermute(
            values, "seq", [(h * ring + z, h * ring + (z + by) % ring) for h in (0, 1) for z in range(ring)]
        )

    def swap(values):
        return lax.ppermute(values, "seq", [(r, (r + ring) % seq_size) for r in range(seq_size)])

    up, down, far = around(near, 1), around(near, -1), swap(near)
    across = around(up, 1)
    own, up, down, far, across = lax.optimization_barrier((own, up, down, far, across))
    other = lax.ppermute(own, "res", [(c, c ^ 1) for c in range(res_size)])
    near_biases = [near, up, down, across]
    far_biases = [far, around(far, 1), around(far, -1), swap(across)]

    mixed = row_attention(place, own, other, near_biases, [], 0, residues, seq_size, head_size)
    columns = lax.all_to_all(columns, "seq", 0, 0)
    mixed, columns = lax.optimization_barrier((mixed, columns))
    mixed = row_attention(place, own, other, far_biases, [mixed], 1, residues, seq_size, head_size)
    mixed = mixed.reshape((seq_size * ring * 2,) + mixed.shape[2:])
    mixed = lax.all_to_all(mixed, ("seq", "res"), 0, 0, axis_index_groups=parity_all)
    mixed = mixed.reshape((seq_size, heads) + mixed.shape[1:])

    params = [
        horizontal_scaling_factor[None],
        horizontal_projection_matrix[:, 3 * channels :],
        horizontal_sigmoid_shift[None],
        horizontal_result_matrix,
        horizontal_result_shift[None],
        downward_stretch_vector[None],
        vertical_projection_matrix,
        vertical_sigmoid_shift[None],
        vertical_result_matrix,
        vertical_result_shift[None],
        feedforward_scaling_factor[None],
        feedforward_expand_matrix,
        feedforward_shrink_matrix,
    ]
    updated = column_phase(mixed, columns, params, heads, scale, span)
    updated = lax.all_to_all(updated, "seq", 0, 0)
    return jnp.transpose(updated.reshape(residues, lines, channels), (1, 0, 2))


def solution(mesh):
    table = P("seq", "res", None)
    return jax.shard_map(
        functools.partial(shards, mesh.shape["seq"], mesh.shape["res"]),
        mesh=mesh,
        in_specs=(table, table, P("seq", "res"), P("res")) + (P(),) * 15,
        out_specs=table,
        check_vma=False,
    )
```

profile of v0, /device:TPU:0, one launch (start us, length us, event | category | flops | bytes accessed | tf_op | source)
XLA Modules:
  0.0 198.8 jit_solution(3021462999372384204)
XLA Ops:
  0.0 1.4 copy.23.head_ref
  1.4 11.5 %pair_bias.1 = bf16[8,10,40,128]{3,2,1,0:T(8,128)(2,1)} custom-call(bf16[320,160,128]{2,1,0:T(8,128)(2,1)} %pair_ref.1, f32[1,128]{1,0:T(1,128)} %bitcast.46, bf16[128,8]{1,0:T(8,128)(2,1)} %copy.23.head_ref), custom_call_target="tpu_custom_call" | custom-call | tf_op jit(solution)/shard_map/pair_bias/pallas_call | solution.py:85
  12.9 5.6 %all-to-all-start = ((bf16[16,5,40,128]{3,2,1,0:T(8,128)(2,1)}), bf16[16,5,40,128]{3,2,1,0:T(8,128)(2,1)S(1)}, u32[]{:S(2)}, u32[]{:S(2)}) async-start(bf16[16,5,40,128]{3,2,1,0:T(8,128)(2,1)} %bitcast.32), calls=%async_computation | async-start | bytes 1638400 | tf_op jit(solution)/shard_map/all_to_all | solution.py:448
  19.1 0.6 bitcast_bitcast_fusion.mask_ref
  19.7 5.1 %pack_heads.1 = bf16[8,2,496,128]{3,2,1,0:T(8,128)(2,1)} custom-call(bf16[8,160,256]{2,1,0:T(8,128)(2,1)} %table_ref, bf16[2,16,128]{2,1,0:T(8,128)(2,1)} %bitcast_bitcast_fusion.mask_ref, f32[1,256]{1,0:T(1,128)} %bitcast.38, bf16[256,1024]{1,0:T(8,128)(2,1)} %weight_ref.1), custom_call_target="tpu_custom_call" | custom-call | tf_op jit(solution)/shard_map/pack_heads/pallas_call | solution.py:138
  24.9 1.0 pad_maximum_fusion
  25.9 6.7 %all-to-all-done.rest_0_ = bf16[16,5,40,128]{3,2,1,0:T(8,128)(2,1)S(1)} async-done(((bf16[16,5,40,128]{3,2,1,0:T(8,128)(2,1)}), bf16[16,5,40,128]{3,2,1,0:T(8,128)(2,1)S(1)}, u32[]{:S(2)}, u32[]{:S(2)}) %all-to-all-start) | async-done | bytes 819232 | tf_op jit(solution)/shard_map/all_to_all | solution.py:448
  32.6 3.6 %all-to-all-start.1 = ((bf16[8,2,496,128]{3,2,1,0:T(8,128)(2,1)}), bf16[8,2,496,128]{3,2,1,0:T(8,128)(2,1)S(1)}, u32[]{:S(2)}, u32[]{:S(2)}) async-start(bf16[8,2,496,128]{3,2,1,0:T(8,128)(2,1)} %pack_heads.1), calls=%async_computation.1 | async-start | bytes 4063232 | tf_op jit(solution)/shard_map/all_to_all | solution.py:463
  36.2 2.0 collective-permute-start
  38.2 2.2 %collective-permute-start.1 = (bf16[16,5,40,128]{3,2,1,0:T(8,128)(2,1)S(1)}, bf16[16,5,40,128]{3,2,1,0:T(8,128)(2,1)S(1)}, u32[]{:S(2)}, u32[]{:S(2)}) collective-permute-start(bf16[16,5,40,128]{3,2,1,0:T(8,128)(2,1)S(1)} %all-to-all-done.rest_0_), channel_id=1, source_target_pairs={{0,48},{16,0},{32,16},{48,32},{64,112},{80,64},{96,80},{112,96},{1... | collective-permute-start | bytes 2457608 | tf_op jit(solution)/shard_map/ppermute | solution.py:468
  40.4 2.9 %collective-permute-start.2 = (bf16[16,5,40,128]{3,2,1,0:T(8,128)(2,1)S(1)}, bf16[16,5,40,128]{3,2,1,0:T(8,128)(2,1)S(1)}, u32[]{:S(2)}, u32[]{:S(2)}) collective-permute-start(bf16[16,5,40,128]{3,2,1,0:T(8,128)(2,1)S(1)} %all-to-all-done.rest_0_), channel_id=1, source_target_pairs={{0,64},{16,80},{32,96},{48,112},{64,0},{80,16},{96,32},{112,48},{1... | collective-permute-start | bytes 2457608 | tf_op jit(solution)/shard_map/ppermute | solution.py:473
  43.3 15.2 %collective-permute-done.rest_1_ = bf16[16,5,40,128]{3,2,1,0:T(8,128)(2,1)S(1)} collective-permute-done((bf16[16,5,40,128]{3,2,1,0:T(8,128)(2,1)S(1)}, bf16[16,5,40,128]{3,2,1,0:T(8,128)(2,1)S(1)}, u32[]{:S(2)}, u32[]{:S(2)}) %collective-permute-start) | collective-permute-done | bytes 819232 | tf_op jit(solution)/shard_map/ppermute | solution.py:468
  58.5 0.9 copy-done.2
  59.4 0.9 copy-done.4
  60.3 18.9 %collective-permute-done.2.rest_0_ = bf16[16,5,40,128]{3,2,1,0:T(8,128)(2,1)S(1)} collective-permute-done((bf16[16,5,40,128]{3,2,1,0:T(8,128)(2,1)S(1)}, bf16[16,5,40,128]{3,2,1,0:T(8,128)(2,1)S(1)}, u32[]{:S(2)}, u32[]{:S(2)}) %collective-permute-start.2) | collective-permute-done | bytes 819232 | tf_op jit(solution)/shard_map/ppermute | solution.py:473
  79.2 0.9 copy-done
  80.1 2.0 collective-permute-start.5
  82.1 2.2 %collective-permute-start.6 = (bf16[16,5,40,128]{3,2,1,0:T(8,128)(2,1)}, bf16[16,5,40,128]{3,2,1,0:T(8,128)(2,1)}, u32[]{:S(2)}, u32[]{:S(2)}) collective-permute-start(bf16[16,5,40,128]{3,2,1,0:T(8,128)(2,1)} %copy-done), channel_id=1, source_target_pairs={{0,48},{16,0},{32,16},{48,32},{64,112},{80,64},{96,80},{112,96},{1... | collective-permute-start | bytes 2457608 | tf_op jit(solution)/shard_map/ppermute | solution.py:468
  84.3 1.0 collective-permute-start.7
  85.3 5.2 %all-to-all-start.2 = ((bf16[8,21,8,256]{3,2,1,0:T(8,128)(2,1)}), bf16[8,21,8,256]{3,2,1,0:T(8,128)(2,1)}, u32[]{:S(2)}, u32[]{:S(2)}) async-start(bf16[8,21,8,256]{3,2,1,0:T(8,128)(2,1)} %pad_maximum_fusion), calls=%async_computation.2 | async-start | bytes 1376256 | tf_op jit(solution)/shard_map/all_to_all | solution.py:483
  90.5 1.1 copy-done.3
  91.7 1.1 copy-done.5
  92.8 23.0 %row_attention.2.rest_4_ = bf16[8,4,40,128]{3,2,1,0:T(8,128)(2,1)S(1)} custom-call(s32[3]{0:T(128)S(1)} %pad_add_fusion.place_ref, bf16[8,2,496,128]{3,2,1,0:T(8,128)(2,1)S(1)} %all-to-all-done.1.own_ref, bf16[8,2,496,128]{3,2,1,0:T(8,128)(2,1)} %collective-permute-done.4.other_ref, bf16[16,5,40,128]{3,2,1,0:T(8,128)(2,1)S(1)} %all-to-all-done.rest_0_, ...), custom_call_target="tpu_custom_call" | custom-call | flops 6710886400 | bytes 12000000 | tf_op jit(solution)/shard_map/row_attention/pallas_call | solution.py:288
  115.8 1.1 copy-done.1
  117.0 24.5 %row_attention.3 = bf16[8,8,40,128]{3,2,1,0:T(8,128)(2,1)} custom-call(s32[3]{0:T(128)S(1)} %pad_add_fusion.place_ref, bf16[8,2,496,128]{3,2,1,0:T(8,128)(2,1)S(1)} %all-to-all-done.1.own_ref, bf16[8,2,496,128]{3,2,1,0:T(8,128)(2,1)} %collective-permute-done.4.other_ref, bf16[16,5,40,128]{3,2,1,0:T(8,128)(2,1)S(1)} %copy-done.1, ...), custom_call_target="tpu_custom_call" | custom-call | flops 6710886400 | bytes 12000000 | tf_op jit(solution)/shard_map/row_attention/pallas_call | solution.py:288
  141.5 10.8 %all-to-all-start.3 = ((bf16[64,40,128]{2,1,0:T(8,128)(2,1)}), bf16[64,40,128]{2,1,0:T(8,128)(2,1)S(1)}, u32[]{:S(2)}, u32[]{:S(2)}) async-start(bf16[64,40,128]{2,1,0:T(8,128)(2,1)} %bitcast.11), calls=%async_computation.3 | async-start | bytes 1310720 | tf_op jit(solution)/shard_map/all_to_all | solution.py:487
  152.3 1.6 slice.3.row_gate_ref
  153.9 12.4 %all-to-all-done.3 = bf16[64,40,128]{2,1,0:T(8,128)(2,1)S(1)} async-done(((bf16[64,40,128]{2,1,0:T(8,128)(2,1)}), bf16[64,40,128]{2,1,0:T(8,128)(2,1)S(1)}, u32[]{:S(2)}, u32[]{:S(2)}) %all-to-all-start.3) | async-done | bytes 655392 | tf_op jit(solution)/shard_map/all_to_all | solution.py:487
  166.3 0.8 copy-done.7
  167.1 16.2 %column_phase.1 = bf16[8,20,8,256]{3,2,1,0:T(8,128)(2,1)} custom-call(bf16[8,8,40,128]{3,2,1,0:T(8,128)(2,1)} %bitcast.36, bf16[8,21,8,256]{3,2,1,0:T(8,128)(2,1)} %all-to-all-done.2.table_ref.mask_ref, bf16[8,21,8,256]{3,2,1,0:T(8,128)(2,1)} %all-to-all-done.2.table_ref.mask_ref, f32[1,256]{1,0:T(1,128)} %bitcast.39, bf16[256,256]{1,0:T(8,128)(2,1)} %slice.3.row_gate_ref, ...), custom_call_target="tpu_custom_call" | custom-call | tf_op jit(solution)/shard_map/column_phase/pallas_call | solution.py:401
  183.3 14.5 %all_to_all.25 = bf16[8,20,8,256]{3,2,1,0:T(8,128)(2,1)S(1)} all-to-all(bf16[8,20,8,256]{3,2,1,0:T(8,128)(2,1)} %column_phase.1), channel_id=1, replica_groups=mesh['seq'=8,'res'=16] {'seq'}, dimensions={0} | all-to-all | bytes 1310720 | tf_op jit(solution)/shard_map/all_to_all | solution.py:506
  197.8 1.0 copy.32
  (30 shorter events, 0.6 us)
Async XLA Ops:
  12.9 5.7 %copy-start.6 = (bf16[8,160,256]{2,1,0:T(8,128)(2,1)S(1)}, bf16[8,160,256]{2,1,0:T(8,128)(2,1)}, u32[]{:S(2)}) copy-start(bf16[8,160,256]{2,1,0:T(8,128)(2,1)} %table_ref) | copy-start | bytes 1966084
  12.9 6.1 %copy-start.8 = (s32[8,160]{1,0:T(8,128)S(1)}, s32[8,160]{1,0:T(8,128)}, u32[]{:S(2)}) copy-start(s32[8,160]{1,0:T(8,128)} %param.21) | copy-start | bytes 15364
  12.9 6.2 %copy-start.9 = (s32[160]{0:T(256)S(1)}, s32[160]{0:T(256)}, u32[]{:S(2)}) copy-start(s32[160]{0:T(256)} %param.22) | copy-start | bytes 1924
  12.9 19.7 %all-to-all-start = ((bf16[16,5,40,128]{3,2,1,0:T(8,128)(2,1)}), bf16[16,5,40,128]{3,2,1,0:T(8,128)(2,1)S(1)}, u32[]{:S(2)}, u32[]{:S(2)}) async-start(bf16[16,5,40,128]{3,2,1,0:T(8,128)(2,1)} %bitcast.32), calls=%async_computation | async-start | bytes 1638400 | tf_op jit(solution)/shard_map/all_to_all | solution.py:448
  32.6 47.6 %all-to-all-start.1 = ((bf16[8,2,496,128]{3,2,1,0:T(8,128)(2,1)}), bf16[8,2,496,128]{3,2,1,0:T(8,128)(2,1)S(1)}, u32[]{:S(2)}, u32[]{:S(2)}) async-start(bf16[8,2,496,128]{3,2,1,0:T(8,128)(2,1)} %pack_heads.1), calls=%async_computation.1 | async-start | bytes 4063232 | tf_op jit(solution)/shard_map/all_to_all | solution.py:463
  36.2 22.3 %collective-permute-start = (bf16[16,5,40,128]{3,2,1,0:T(8,128)(2,1)S(1)}, bf16[16,5,40,128]{3,2,1,0:T(8,128)(2,1)S(1)}, u32[]{:S(2)}, u32[]{:S(2)}) collective-permute-start(bf16[16,5,40,128]{3,2,1,0:T(8,128)(2,1)S(1)} %all-to-all-done.rest_0_), channel_id=1, source_target_pairs={{0,16},{16,32},{32,48},{48,0},{64,80},{80,96},{96,112},{112,64},{1... | collective-permute-start | bytes 2457608 | tf_op jit(solution)/shard_map/ppermute | solution.py:468
  38.2 21.2 %collective-permute-start.1 = (bf16[16,5,40,128]{3,2,1,0:T(8,128)(2,1)S(1)}, bf16[16,5,40,128]{3,2,1,0:T(8,128)(2,1)S(1)}, u32[]{:S(2)}, u32[]{:S(2)}) collective-permute-start(bf16[16,5,40,128]{3,2,1,0:T(8,128)(2,1)S(1)} %all-to-all-done.rest_0_), channel_id=1, source_target_pairs={{0,48},{16,0},{32,16},{48,32},{64,112},{80,64},{96,80},{112,96},{1... | collective-permute-start | bytes 2457608 | tf_op jit(solution)/shard_map/ppermute | solution.py:468
  40.4 38.9 %collective-permute-start.2 = (bf16[16,5,40,128]{3,2,1,0:T(8,128)(2,1)S(1)}, bf16[16,5,40,128]{3,2,1,0:T(8,128)(2,1)S(1)}, u32[]{:S(2)}, u32[]{:S(2)}) collective-permute-start(bf16[16,5,40,128]{3,2,1,0:T(8,128)(2,1)S(1)} %all-to-all-done.rest_0_), channel_id=1, source_target_pairs={{0,64},{16,80},{32,96},{48,112},{64,0},{80,16},{96,32},{112,48},{1... | collective-permute-start | bytes 2457608 | tf_op jit(solution)/shard_map/ppermute | solution.py:473
  58.5 21.7 %collective-permute-start.3 = (bf16[16,5,40,128]{3,2,1,0:T(8,128)(2,1)S(1)}, bf16[16,5,40,128]{3,2,1,0:T(8,128)(2,1)}, u32[]{:S(2)}, u32[]{:S(2)}) collective-permute-start(bf16[16,5,40,128]{3,2,1,0:T(8,128)(2,1)S(1)} %collective-permute-done.rest_1_), channel_id=1, source_target_pairs={{0,16},{16,32},{32,48},{48,0},{64,80},{80,96},{96,112},{112,64},{1... | collective-permute-start | bytes 2457608 | tf_op jit(solution)/shard_map/ppermute | solution.py:468
  58.5 0.9 copy-start.2
  59.4 0.9 copy-start.4
  79.2 0.9 copy-start
  80.1 10.4 %collective-permute-start.4 = (bf16[8,2,496,128]{3,2,1,0:T(8,128)(2,1)S(1)}, bf16[8,2,496,128]{3,2,1,0:T(8,128)(2,1)}, u32[]{:S(2)}, u32[]{:S(2)}) collective-permute-start(bf16[8,2,496,128]{3,2,1,0:T(8,128)(2,1)S(1)} %all-to-all-done.1.own_ref), channel_id=1, source_target_pairs={{0,1},{1,0},{2,3},{3,2},{4,5},{5,4},{6,7},{7,6},{8,9},{9,8},{10,11... | collective-permute-start | bytes 6094856 | tf_op jit(solution)/shard_map/ppermute | solution.py:478
  80.1 35.7 %collective-permute-start.5 = (bf16[16,5,40,128]{3,2,1,0:T(8,128)(2,1)}, bf16[16,5,40,128]{3,2,1,0:T(8,128)(2,1)}, u32[]{:S(2)}, u32[]{:S(2)}) collective-permute-start(bf16[16,5,40,128]{3,2,1,0:T(8,128)(2,1)} %copy-done), channel_id=1, source_target_pairs={{0,16},{16,32},{32,48},{48,0},{64,80},{80,96},{96,112},{112,64},{1... | collective-permute-start | bytes 2457608 | tf_op jit(solution)/shard_map/ppermute | solution.py:468
  82.1 33.7 %collective-permute-start.6 = (bf16[16,5,40,128]{3,2,1,0:T(8,128)(2,1)}, bf16[16,5,40,128]{3,2,1,0:T(8,128)(2,1)}, u32[]{:S(2)}, u32[]{:S(2)}) collective-permute-start(bf16[16,5,40,128]{3,2,1,0:T(8,128)(2,1)} %copy-done), channel_id=1, source_target_pairs={{0,48},{16,0},{32,16},{48,32},{64,112},{80,64},{96,80},{112,96},{1... | collective-permute-start | bytes 2457608 | tf_op jit(solution)/shard_map/ppermute | solution.py:468
  84.3 31.5 %collective-permute-start.7 = (bf16[16,5,40,128]{3,2,1,0:T(8,128)(2,1)}, bf16[16,5,40,128]{3,2,1,0:T(8,128)(2,1)}, u32[]{:S(2)}, u32[]{:S(2)}) collective-permute-start(bf16[16,5,40,128]{3,2,1,0:T(8,128)(2,1)} %collective-permute-done.3.rest_3_), channel_id=1, source_target_pairs={{0,64},{16,80},{32,96},{48,112},{64,0},{80,16},{96,32},{112,48},{1... | collective-permute-start | bytes 2457608 | tf_op jit(solution)/shard_map/ppermute | solution.py:473
  85.3 30.5 %all-to-all-start.2 = ((bf16[8,21,8,256]{3,2,1,0:T(8,128)(2,1)}), bf16[8,21,8,256]{3,2,1,0:T(8,128)(2,1)}, u32[]{:S(2)}, u32[]{:S(2)}) async-start(bf16[8,21,8,256]{3,2,1,0:T(8,128)(2,1)} %pad_maximum_fusion), calls=%async_computation.2 | async-start | bytes 1376256 | tf_op jit(solution)/shard_map/all_to_all | solution.py:483
  90.5 1.1 copy-start.3
  91.7 1.1 copy-start.5
  115.8 1.1 copy-start.1
  141.5 24.8 %all-to-all-start.3 = ((bf16[64,40,128]{2,1,0:T(8,128)(2,1)}), bf16[64,40,128]{2,1,0:T(8,128)(2,1)S(1)}, u32[]{:S(2)}, u32[]{:S(2)}) async-start(bf16[64,40,128]{2,1,0:T(8,128)(2,1)} %bitcast.11), calls=%async_computation.3 | async-start | bytes 1310720 | tf_op jit(solution)/shard_map/all_to_all | solution.py:487
  166.3 0.8 copy-start.7
where the time goes:
time: 200 us; the launch traced here: 199 us
  Pallas kernels  80.3 us (40%)
  waiting for transfers between devices  53.2 us (27%)
  starting transfers between devices  37.5 us (19%)
  blocking collectives  14.5 us (7%)
  local copies, waits for them, and re-layouts  12 us (6%)
    pallas_call x2, Pallas kernels, row_attention(): pl.pallas_call(functools.partial(row_kernel, turn=turn, count=count, resi...  47.5 us
    ppermute x2, waiting for transfers between devices, swap(): lax.ppermute(values, 'seq', [(r, (r + ring) % seq_size) for r in range(se...  18.9 us
    pallas_call x1, Pallas kernels, column_phase(): pl.pallas_call(functools.partial(column_kernel, heads=heads, scale=scale)...  16.2 us
    ppermute x5, waiting for transfers between devices, around(): lax.ppermute(values, 'seq', [(h * ring + z, h * ring + (z + by) % ring) f...  15.2 us
    all_to_all x1, blocking collectives, shards(): updated = lax.all_to_all(updated, 'seq', 0, 0)  14.5 us
    all_to_all x1, waiting for transfers between devices, shards(): lax.all_to_all(mixed, ('seq', 'res'), 0, 0, axis_index_groups=parity_all)  12.4 us
    pallas_call x1, Pallas kernels, pair_bias(): pl.pallas_call(pair_kernel, grid=(rows // STEP,), in_specs=[pl.BlockSpec(...  11.5 us
    all_to_all x1, starting transfers between devices, shards(): lax.all_to_all(mixed, ('seq', 'res'), 0, 0, axis_index_groups=parity_all)  10.8 us
  transfers between devices with their start and end apart: 12, of which 4 were waited for; matrix products, arithmetic and copies ran while one was open for 2% of the time, Pallas kernels for 14%

commit v1 on v0

--- a/solution.py
+++ b/solution.py
@@ -15,7 +15,7 @@
 LANES = 128
 MASKED = -1e30
 VMEM = 56 * 2**20
-ROW_VMEM = 40 * 2**20
+LESS_VMEM = 40 * 2**20
 
 
 def dot(a, b):
@@ -67,34 +67,37 @@
         raw = both[channels : channels + heads] + both[channels + heads :]
         return raw * lax.rsqrt(spread + EPS)
 
-    for i in range(0, STEP, 2):
-        done = project(pair_ref[i : i + 2, :LANES, :].reshape(2 * LANES, channels))
-        rows_ref[:, i, :] = done[:, :LANES]
-        rows_ref[:, i + 1, :] = done[:, LANES:]
-    for r in range(0, EIGHT, 2):
-        rest = [pair_ref[g * EIGHT + r + e, LANES:, :] for e in range(2) for g in range(GROUPS)]
-        done = project(jnp.concatenate(rest, axis=0))
-        rows_ref[:, STEP + r, :] = done[:, :LANES]
-        rows_ref[:, STEP + r + 1, :] = done[:, LANES:]
-    bias_ref[:, 0] = rows_ref[...].astype(BF16)
-
-
-def pair_bias(coupled, gain, head_matrix):
+    for part in range(bias_ref.shape[1]):
+        row, at = part * STEP, part * STEP_ROWS
+        for i in range(0, STEP, 2):
+            done = project(pair_ref[row + i : row + i + 2, :LANES, :].reshape(2 * LANES, channels))
+            rows_ref[:, at + i, :] = done[:, :LANES]
+            rows_ref[:, at + i + 1, :] = done[:, LANES:]
+        for r in range(0, EIGHT, 2):
+            rest = [pair_ref[row + g * EIGHT + r + e, LANES:, :] for e in range(2) for g in range(GROUPS)]
+            done = project(jnp.concatenate(rest, axis=0))
+            rows_ref[:, at + STEP + r, :] = done[:, :LANES]
+            rows_ref[:, at + STEP + r + 1, :] = done[:, LANES:]
+    for part in range(bias_ref.shape[1]):
+        bias_ref[:, part] = rows_ref[:, part * STEP_ROWS : (part + 1) * STEP_ROWS].astype(BF16)
+
+
+def pair_bias(coupled, gain, head_matrix, parts):
     rows, cols, channels = coupled.shape
     heads = head_matrix.shape[1]
     return pl.pallas_call(
         pair_kernel,
-        grid=(rows // STEP,),
+        grid=(rows // STEP // parts,),
         in_specs=[
-            pl.BlockSpec((STEP, cols, channels), lambda i: (i, 0, 0)),
+            pl.BlockSpec((parts * STEP, cols, channels), lambda i: (i, 0, 0)),
             pl.BlockSpec((1, channels), lambda i: (0, 0)),
             pl.BlockSpec((channels, heads), lambda i: (0, 0)),
         ],
-        out_specs=pl.BlockSpec((heads, 1, STEP_ROWS, LANES), lambda i: (0, i, 0, 0)),
+        out_specs=pl.BlockSpec((heads, parts, STEP_ROWS, LANES), lambda i: (0, i, 0, 0)),
         out_shape=jax.ShapeDtypeStruct((heads, rows // STEP, STEP_ROWS, LANES), BF16),
         scratch_shapes=[
             pltpu.VMEM((channels + 2 * heads, channels), BF16),
-            pltpu.VMEM((heads, STEP_ROWS, LANES), F32),
+            pltpu.VMEM((heads, parts * STEP_ROWS, LANES), F32),
         ],
         compiler_params=pltpu.CompilerParams(vmem_limit_bytes=VMEM),
         name="pair_bias",
@@ -298,7 +301,7 @@
             pltpu.VMEM((2, residues, keys), F32),
             pltpu.VMEM((2, residues, keys), BF16),
         ],
-        compiler_params=pltpu.CompilerParams(vmem_limit_bytes=ROW_VMEM),
+        compiler_params=pltpu.CompilerParams(vmem_limit_bytes=LESS_VMEM),
         cost_estimate=pl.CostEstimate(flops=scores * 512, bytes_accessed=12_000_000, transcendentals=scores),
         name="row_attention",
     )(place, own, other, *biases, *earlier)
@@ -405,7 +408,7 @@
         out_specs=token_block,
         out_shape=jax.ShapeDtypeStruct((groups, residues, lines, channels), BF16),
         scratch_shapes=[pltpu.VMEM((channels // LANES, residues * groups * lines, LANES), F32)],
-        compiler_params=pltpu.CompilerParams(vmem_limit_bytes=VMEM),
+        compiler_params=pltpu.CompilerParams(vmem_limit_bytes=LESS_VMEM),
         name="column_phase",
     )(mixed, table, table, *params)
 
@@ -442,7 +445,7 @@
     parity = [list(range(p, res_size, 2)) for p in (0, 1)]
     parity_all = [[r * res_size + c for r in range(seq_size) for c in group] for group in parity]
 
-    tile_bias = pair_bias(coupled_state, coupling_scaling_factor, coupling_head_matrix)
+    tile_bias = pair_bias(coupled_state, coupling_scaling_factor, coupling_head_matrix, residues // STEP)
     tile_bias, homology_table = lax.optimization_barrier((tile_bias, homology_table))
     steps = tile_bias.shape[1] // 2
     near = lax.all_to_all(tile_bias.reshape(res_size, steps, STEP_ROWS, LANES), "res", 0, 0)

time: 200 us -> 196 us (0.980)
  Pallas kernels: 80.3 us -> 74.2 us
  local copies, waits for them, and re-layouts: 12 us -> 14.4 us
    pallas_call x1, Pallas kernels: 11.5 us -> 8.17 us  [pair_bias(): pl.pallas_call(pair_kernel, grid=(rows // STEP // parts,), in_specs=[pl.B...]
    unnamed x21 -> x47, local copies, waits for them, and re-layouts: 8.37 us -> 11.4 us
    pallas_call x1, Pallas kernels: 16.2 us -> 13.4 us  [column_phase(): pl.pallas_call(functools.partial(column_kernel, heads=heads, scale=scale)...]
where the time goes in v1:
time: 196 us; the launch traced here: 195 us
  Pallas kernels  74.2 us (38%)
  waiting for transfers between devices  53.8 us (27%)
  starting transfers between devices  37.5 us (19%)
  local copies, waits for them, and re-layouts  14.4 us (7%)
  blocking collectives  13.5 us (7%)
    pallas_call x2, Pallas kernels, row_attention(): pl.pallas_call(functools.partial(row_kernel, turn=turn, count=count, resi...  47.5 us
    ppermute x2, waiting for transfers between devices, swap(): lax.ppermute(values, 'seq', [(r, (r + ring) % seq_size) for r in range(se...  18.9 us
    ppermute x5, waiting for transfers between devices, around(): lax.ppermute(values, 'seq', [(h * ring + z, h * ring + (z + by) % ring) f...  15.2 us
    all_to_all x1, blocking collectives, shards(): updated = lax.all_to_all(updated, 'seq', 0, 0)  13.5 us
    pallas_call x1, Pallas kernels, column_phase(): pl.pallas_call(functools.partial(column_kernel, heads=heads, scale=scale)...  13.4 us
    all_to_all x1, waiting for transfers between devices, shards(): lax.all_to_all(mixed, ('seq', 'res'), 0, 0, axis_index_groups=parity_all)  13 us
    unnamed x47, local copies, waits for them, and re-layouts  11.4 us
    all_to_all x1, starting transfers between devices, shards(): lax.all_to_all(mixed, ('seq', 'res'), 0, 0, axis_index_groups=parity_all)  10.8 us
  transfers between devices with their start and end apart: 12, of which 4 were waited for; matrix products, arithmetic and copies ran while one was open for 2% of the time, Pallas kernels for 14%

profile of v1, /device:TPU:0, one launch (start us, length us, event | category | flops | bytes accessed | tf_op | source)
XLA Modules:
  0.0 194.9 jit_solution(10129403392762892074)
XLA Ops:
  0.0 1.4 copy.23.head_ref
  1.4 8.2 %pair_bias.1 = bf16[8,10,40,128]{3,2,1,0:T(8,128)(2,1)} custom-call(bf16[320,160,128]{2,1,0:T(8,128)(2,1)} %pair_ref.1, f32[1,128]{1,0:T(1,128)} %bitcast.46, bf16[128,8]{1,0:T(8,128)(2,1)} %copy.23.head_ref), custom_call_target="tpu_custom_call" | custom-call | tf_op jit(solution)/shard_map/pair_bias/pallas_call | solution.py:88
  9.6 5.6 %all-to-all-start = ((bf16[16,5,40,128]{3,2,1,0:T(8,128)(2,1)}), bf16[16,5,40,128]{3,2,1,0:T(8,128)(2,1)S(1)}, u32[]{:S(2)}, u32[]{:S(2)}) async-start(bf16[16,5,40,128]{3,2,1,0:T(8,128)(2,1)} %bitcast.41), calls=%async_computation | async-start | bytes 1638400 | tf_op jit(solution)/shard_map/all_to_all | solution.py:451
  16.4 5.1 %pack_heads.1 = bf16[8,2,496,128]{3,2,1,0:T(8,128)(2,1)} custom-call(bf16[8,160,256]{2,1,0:T(8,128)(2,1)} %table_ref, bf16[2,16,128]{2,1,0:T(8,128)(2,1)} %bitcast_bitcast_fusion.mask_ref, f32[1,256]{1,0:T(1,128)} %bitcast.33, bf16[256,1024]{1,0:T(8,128)(2,1)} %weight_ref.1), custom_call_target="tpu_custom_call" | custom-call | tf_op jit(solution)/shard_map/pack_heads/pallas_call | solution.py:141
  21.6 1.0 pad_maximum_fusion
  22.6 6.7 %all-to-all-done.rest_0_ = bf16[16,5,40,128]{3,2,1,0:T(8,128)(2,1)S(1)} async-done(((bf16[16,5,40,128]{3,2,1,0:T(8,128)(2,1)}), bf16[16,5,40,128]{3,2,1,0:T(8,128)(2,1)S(1)}, u32[]{:S(2)}, u32[]{:S(2)}) %all-to-all-start) | async-done | bytes 819232 | tf_op jit(solution)/shard_map/all_to_all | solution.py:451
  29.2 3.6 %all-to-all-start.1 = ((bf16[8,2,496,128]{3,2,1,0:T(8,128)(2,1)}), bf16[8,2,496,128]{3,2,1,0:T(8,128)(2,1)S(1)}, u32[]{:S(2)}, u32[]{:S(2)}) async-start(bf16[8,2,496,128]{3,2,1,0:T(8,128)(2,1)} %pack_heads.1), calls=%async_computation.1 | async-start | bytes 4063232 | tf_op jit(solution)/shard_map/all_to_all | solution.py:466
  32.9 2.0 %collective-permute-start = (bf16[16,5,40,128]{3,2,1,0:T(8,128)(2,1)S(1)}, bf16[16,5,40,128]{3,2,1,0:T(8,128)(2,1)S(1)}, u32[]{:S(2)}, u32[]{:S(2)}) collective-permute-start(bf16[16,5,40,128]{3,2,1,0:T(8,128)(2,1)S(1)} %all-to-all-done.rest_0_), channel_id=1, source_target_pairs={{0,16},{16,32},{32,48},{48,0},{64,80},{80,96},{96,112},{112,64},{1... | collective-permute-start | bytes 2457608 | tf_op jit(solution)/shard_map/ppermute | solution.py:471
  34.8 2.2 %collective-permute-start.1 = (bf16[16,5,40,128]{3,2,1,0:T(8,128)(2,1)S(1)}, bf16[16,5,40,128]{3,2,1,0:T(8,128)(2,1)S(1)}, u32[]{:S(2)}, u32[]{:S(2)}) collective-permute-start(bf16[16,5,40,128]{3,2,1,0:T(8,128)(2,1)S(1)} %all-to-all-done.rest_0_), channel_id=1, source_target_pairs={{0,48},{16,0},{32,16},{48,32},{64,112},{80,64},{96,80},{112,96},{1... | collective-permute-start | bytes 2457608 | tf_op jit(solution)/shard_map/ppermute | solution.py:471
  37.0 2.9 %collective-permute-start.2 = (bf16[16,5,40,128]{3,2,1,0:T(8,128)(2,1)S(1)}, bf16[16,5,40,128]{3,2,1,0:T(8,128)(2,1)S(1)}, u32[]{:S(2)}, u32[]{:S(2)}) collective-permute-start(bf16[16,5,40,128]{3,2,1,0:T(8,128)(2,1)S(1)} %all-to-all-done.rest_0_), channel_id=1, source_target_pairs={{0,64},{16,80},{32,96},{48,112},{64,0},{80,16},{96,32},{112,48},{1... | collective-permute-start | bytes 2457608 | tf_op jit(solution)/shard_map/ppermute | solution.py:476
  39.9 15.2 %collective-permute-done.rest_1_ = bf16[16,5,40,128]{3,2,1,0:T(8,128)(2,1)S(1)} collective-permute-done((bf16[16,5,40,128]{3,2,1,0:T(8,128)(2,1)S(1)}, bf16[16,5,40,128]{3,2,1,0:T(8,128)(2,1)S(1)}, u32[]{:S(2)}, u32[]{:S(2)}) %collective-permute-start) | collective-permute-done | bytes 819232 | tf_op jit(solution)/shard_map/ppermute | solution.py:471
  56.1 0.9 copy-done.16
  57.0 18.9 %collective-permute-done.2.rest_0_ = bf16[16,5,40,128]{3,2,1,0:T(8,128)(2,1)S(1)} collective-permute-done((bf16[16,5,40,128]{3,2,1,0:T(8,128)(2,1)S(1)}, bf16[16,5,40,128]{3,2,1,0:T(8,128)(2,1)S(1)}, u32[]{:S(2)}, u32[]{:S(2)}) %collective-permute-start.2) | collective-permute-done | bytes 819232 | tf_op jit(solution)/shard_map/ppermute | solution.py:476
  75.9 0.9 copy-done.12
  76.8 2.0 %collective-permute-start.5 = (bf16[16,5,40,128]{3,2,1,0:T(8,128)(2,1)}, bf16[16,5,40,128]{3,2,1,0:T(8,128)(2,1)}, u32[]{:S(2)}, u32[]{:S(2)}) collective-permute-start(bf16[16,5,40,128]{3,2,1,0:T(8,128)(2,1)} %copy-done.12), channel_id=1, source_target_pairs={{0,16},{16,32},{32,48},{48,0},{64,80},{80,96},{96,112},{112,64},{1... | collective-permute-start | bytes 2457608 | tf_op jit(solution)/shard_map/ppermute | solution.py:471
  78.8 2.2 %collective-permute-start.6 = (bf16[16,5,40,128]{3,2,1,0:T(8,128)(2,1)}, bf16[16,5,40,128]{3,2,1,0:T(8,128)(2,1)}, u32[]{:S(2)}, u32[]{:S(2)}) collective-permute-start(bf16[16,5,40,128]{3,2,1,0:T(8,128)(2,1)} %copy-done.12), channel_id=1, source_target_pairs={{0,48},{16,0},{32,16},{48,32},{64,112},{80,64},{96,80},{112,96},{1... | collective-permute-start | bytes 2457608 | tf_op jit(solution)/shard_map/ppermute | solution.py:471
  81.0 0.9 collective-permute-start.7
  82.0 5.2 %all-to-all-start.2 = ((bf16[8,21,8,256]{3,2,1,0:T(8,128)(2,1)}), bf16[8,21,8,256]{3,2,1,0:T(8,128)(2,1)S(1)}, u32[]{:S(2)}, u32[]{:S(2)}) async-start(bf16[8,21,8,256]{3,2,1,0:T(8,128)(2,1)} %pad_maximum_fusion), calls=%async_computation.2 | async-start | bytes 1376256 | tf_op jit(solution)/shard_map/all_to_all | solution.py:486
  87.2 1.1 copy-done.15
  88.4 1.1 copy-done.17
  89.5 23.0 %row_attention.2.rest_4_ = bf16[8,4,40,128]{3,2,1,0:T(8,128)(2,1)S(1)} custom-call(s32[3]{0:T(128)S(1)} %pad_add_fusion.place_ref, bf16[8,2,496,128]{3,2,1,0:T(8,128)(2,1)S(1)} %all-to-all-done.1.own_ref, bf16[8,2,496,128]{3,2,1,0:T(8,128)(2,1)} %collective-permute-done.4.other_ref, bf16[16,5,40,128]{3,2,1,0:T(8,128)(2,1)S(1)} %all-to-all-done.rest_0_, ...), custom_call_target="tpu_custom_call" | custom-call | flops 6710886400 | bytes 12000000 | tf_op jit(solution)/shard_map/row_attention/pallas_call | solution.py:291
  113.4 1.2 copy-done.13
  114.6 1.0 copy-done.19
  115.5 24.5 %row_attention.3 = bf16[8,8,40,128]{3,2,1,0:T(8,128)(2,1)} custom-call(s32[3]{0:T(128)S(1)} %pad_add_fusion.place_ref, bf16[8,2,496,128]{3,2,1,0:T(8,128)(2,1)S(1)} %all-to-all-done.1.own_ref, bf16[8,2,496,128]{3,2,1,0:T(8,128)(2,1)} %collective-permute-done.4.other_ref, bf16[16,5,40,128]{3,2,1,0:T(8,128)(2,1)S(1)} %copy-done.13, ...), custom_call_target="tpu_custom_call" | custom-call | flops 6710886400 | bytes 12000000 | tf_op jit(solution)/shard_map/row_attention/pallas_call | solution.py:291
  140.0 10.8 %all-to-all-start.3 = ((bf16[64,40,128]{2,1,0:T(8,128)(2,1)}), bf16[64,40,128]{2,1,0:T(8,128)(2,1)S(1)}, u32[]{:S(2)}, u32[]{:S(2)}) async-start(bf16[64,40,128]{2,1,0:T(8,128)(2,1)} %bitcast.11), calls=%async_computation.3 | async-start | bytes 1310720 | tf_op jit(solution)/shard_map/all_to_all | solution.py:490
  150.9 0.9 slice.3.row_gate_ref
  151.8 13.0 %all-to-all-done.3 = bf16[64,40,128]{2,1,0:T(8,128)(2,1)S(1)} async-done(((bf16[64,40,128]{2,1,0:T(8,128)(2,1)}), bf16[64,40,128]{2,1,0:T(8,128)(2,1)S(1)}, u32[]{:S(2)}, u32[]{:S(2)}) %all-to-all-start.3) | async-done | bytes 655392 | tf_op jit(solution)/shard_map/all_to_all | solution.py:490
  164.9 1.0 copy-done.1
  165.9 1.0 copy-done.2
  167.0 13.4 %column_phase.1 = bf16[8,20,8,256]{3,2,1,0:T(8,128)(2,1)S(1)} custom-call(bf16[8,8,40,128]{3,2,1,0:T(8,128)(2,1)S(1)} %bitcast.32, bf16[8,21,8,256]{3,2,1,0:T(8,128)(2,1)S(1)} %all-to-all-done.2.table_ref.mask_ref, bf16[8,21,8,256]{3,2,1,0:T(8,128)(2,1)S(1)} %all-to-all-done.2.table_ref.mask_ref, f32[1,256]{1,0:T(1,128)S(1)} %bitcast.34, ...), custom_call_target="tpu_custom_call" | custom-call | tf_op jit(solution)/shard_map/column_phase/pallas_call | solution.py:404
  180.4 13.5 %all_to_all.25 = bf16[8,20,8,256]{3,2,1,0:T(8,128)(2,1)S(1)} all-to-all(bf16[8,20,8,256]{3,2,1,0:T(8,128)(2,1)S(1)} %column_phase.1), channel_id=1, replica_groups=mesh['seq'=8,'res'=16] {'seq'}, dimensions={0} | all-to-all | bytes 1310720 | tf_op jit(solution)/shard_map/all_to_all | solution.py:509
  193.9 1.0 copy.32
  (56 shorter events, 2.9 us)
Async XLA Ops:
  9.6 5.7 %copy-start.20 = (bf16[8,160,256]{2,1,0:T(8,128)(2,1)S(1)}, bf16[8,160,256]{2,1,0:T(8,128)(2,1)}, u32[]{:S(2)}) copy-start(bf16[8,160,256]{2,1,0:T(8,128)(2,1)} %table_ref) | copy-start | bytes 1966084
  9.6 6.1 %copy-start.21 = (s32[8,160]{1,0:T(8,128)S(1)}, s32[8,160]{1,0:T(8,128)}, u32[]{:S(2)}) copy-start(s32[8,160]{1,0:T(8,128)} %param.21) | copy-start | bytes 15364
  9.6 6.2 %copy-start.22 = (s32[160]{0:T(256)S(1)}, s32[160]{0:T(256)}, u32[]{:S(2)}) copy-start(s32[160]{0:T(256)} %param.22) | copy-start | bytes 1924
  9.6 19.7 %all-to-all-start = ((bf16[16,5,40,128]{3,2,1,0:T(8,128)(2,1)}), bf16[16,5,40,128]{3,2,1,0:T(8,128)(2,1)S(1)}, u32[]{:S(2)}, u32[]{:S(2)}) async-start(bf16[16,5,40,128]{3,2,1,0:T(8,128)(2,1)} %bitcast.41), calls=%async_computation | async-start | bytes 1638400 | tf_op jit(solution)/shard_map/all_to_all | solution.py:451
  29.2 47.6 %all-to-all-start.1 = ((bf16[8,2,496,128]{3,2,1,0:T(8,128)(2,1)}), bf16[8,2,496,128]{3,2,1,0:T(8,128)(2,1)S(1)}, u32[]{:S(2)}, u32[]{:S(2)}) async-start(bf16[8,2,496,128]{3,2,1,0:T(8,128)(2,1)} %pack_heads.1), calls=%async_computation.1 | async-start | bytes 4063232 | tf_op jit(solution)/shard_map/all_to_all | solution.py:466
  32.9 22.3 %collective-permute-start = (bf16[16,5,40,128]{3,2,1,0:T(8,128)(2,1)S(1)}, bf16[16,5,40,128]{3,2,1,0:T(8,128)(2,1)S(1)}, u32[]{:S(2)}, u32[]{:S(2)}) collective-permute-start(bf16[16,5,40,128]{3,2,1,0:T(8,128)(2,1)S(1)} %all-to-all-done.rest_0_), channel_id=1, source_target_pairs={{0,16},{16,32},{32,48},{48,0},{64,80},{80,96},{96,112},{112,64},{1... | collective-permute-start | bytes 2457608 | tf_op jit(solution)/shard_map/ppermute | solution.py:471
  34.8 21.2 %collective-permute-start.1 = (bf16[16,5,40,128]{3,2,1,0:T(8,128)(2,1)S(1)}, bf16[16,5,40,128]{3,2,1,0:T(8,128)(2,1)S(1)}, u32[]{:S(2)}, u32[]{:S(2)}) collective-permute-start(bf16[16,5,40,128]{3,2,1,0:T(8,128)(2,1)S(1)} %all-to-all-done.rest_0_), channel_id=1, source_target_pairs={{0,48},{16,0},{32,16},{48,32},{64,112},{80,64},{96,80},{112,96},{1... | collective-permute-start | bytes 2457608 | tf_op jit(solution)/shard_map/ppermute | solution.py:471
  37.0 38.9 %collective-permute-start.2 = (bf16[16,5,40,128]{3,2,1,0:T(8,128)(2,1)S(1)}, bf16[16,5,40,128]{3,2,1,0:T(8,128)(2,1)S(1)}, u32[]{:S(2)}, u32[]{:S(2)}) collective-permute-start(bf16[16,5,40,128]{3,2,1,0:T(8,128)(2,1)S(1)} %all-to-all-done.rest_0_), channel_id=1, source_target_pairs={{0,64},{16,80},{32,96},{48,112},{64,0},{80,16},{96,32},{112,48},{1... | collective-permute-start | bytes 2457608 | tf_op jit(solution)/shard_map/ppermute | solution.py:476
  55.2 21.7 %collective-permute-start.3 = (bf16[16,5,40,128]{3,2,1,0:T(8,128)(2,1)S(1)}, bf16[16,5,40,128]{3,2,1,0:T(8,128)(2,1)}, u32[]{:S(2)}, u32[]{:S(2)}) collective-permute-start(bf16[16,5,40,128]{3,2,1,0:T(8,128)(2,1)S(1)} %collective-permute-done.rest_1_), channel_id=1, source_target_pairs={{0,16},{16,32},{32,48},{48,0},{64,80},{80,96},{96,112},{112,64},{1... | collective-permute-start | bytes 2457608 | tf_op jit(solution)/shard_map/ppermute | solution.py:471
  75.9 0.9 copy-start.12
  76.8 10.4 %collective-permute-start.4 = (bf16[8,2,496,128]{3,2,1,0:T(8,128)(2,1)S(1)}, bf16[8,2,496,128]{3,2,1,0:T(8,128)(2,1)}, u32[]{:S(2)}, u32[]{:S(2)}) collective-permute-start(bf16[8,2,496,128]{3,2,1,0:T(8,128)(2,1)S(1)} %all-to-all-done.1.own_ref), channel_id=1, source_target_pairs={{0,1},{1,0},{2,3},{3,2},{4,5},{5,4},{6,7},{7,6},{8,9},{9,8},{10,11... | collective-permute-start | bytes 6094856 | tf_op jit(solution)/shard_map/ppermute | solution.py:481
  76.8 36.5 %collective-permute-start.5 = (bf16[16,5,40,128]{3,2,1,0:T(8,128)(2,1)}, bf16[16,5,40,128]{3,2,1,0:T(8,128)(2,1)}, u32[]{:S(2)}, u32[]{:S(2)}) collective-permute-start(bf16[16,5,40,128]{3,2,1,0:T(8,128)(2,1)} %copy-done.12), channel_id=1, source_target_pairs={{0,16},{16,32},{32,48},{48,0},{64,80},{80,96},{96,112},{112,64},{1... | collective-permute-start | bytes 2457608 | tf_op jit(solution)/shard_map/ppermute | solution.py:471
  78.8 34.5 %collective-permute-start.6 = (bf16[16,5,40,128]{3,2,1,0:T(8,128)(2,1)}, bf16[16,5,40,128]{3,2,1,0:T(8,128)(2,1)}, u32[]{:S(2)}, u32[]{:S(2)}) collective-permute-start(bf16[16,5,40,128]{3,2,1,0:T(8,128)(2,1)} %copy-done.12), channel_id=1, source_target_pairs={{0,48},{16,0},{32,16},{48,32},{64,112},{80,64},{96,80},{112,96},{1... | collective-permute-start | bytes 2457608 | tf_op jit(solution)/shard_map/ppermute | solution.py:471
  81.0 32.3 %collective-permute-start.7 = (bf16[16,5,40,128]{3,2,1,0:T(8,128)(2,1)}, bf16[16,5,40,128]{3,2,1,0:T(8,128)(2,1)}, u32[]{:S(2)}, u32[]{:S(2)}) collective-permute-start(bf16[16,5,40,128]{3,2,1,0:T(8,128)(2,1)} %collective-permute-done.3.rest_3_), channel_id=1, source_target_pairs={{0,64},{16,80},{32,96},{48,112},{64,0},{80,16},{96,32},{112,48},{1... | collective-permute-start | bytes 2457608 | tf_op jit(solution)/shard_map/ppermute | solution.py:476
  82.0 31.3 %all-to-all-start.2 = ((bf16[8,21,8,256]{3,2,1,0:T(8,128)(2,1)}), bf16[8,21,8,256]{3,2,1,0:T(8,128)(2,1)S(1)}, u32[]{:S(2)}, u32[]{:S(2)}) async-start(bf16[8,21,8,256]{3,2,1,0:T(8,128)(2,1)} %pad_maximum_fusion), calls=%async_computation.2 | async-start | bytes 1376256 | tf_op jit(solution)/shard_map/all_to_all | solution.py:486
  87.2 1.1 copy-start.15
  88.4 1.1 copy-start.17
  113.2 51.6 %copy-start = (bf16[256,1024]{1,0:T(8,128)(2,1)S(1)}, bf16[256,1024]{1,0:T(8,128)(2,1)}, u32[]{:S(2)}) copy-start(bf16[256,1024]{1,0:T(8,128)(2,1)} %col_weight_ref.1) | copy-start | bytes 1572868
  113.2 51.6 %copy-start.3 = (bf16[256,256]{1,0:T(8,128)(2,1)S(1)}, bf16[256,256]{1,0:T(8,128)(2,1)}, u32[]{:S(2)}) copy-start(bf16[256,256]{1,0:T(8,128)(2,1)} %row_out_ref.1) | copy-start | bytes 393220
  113.2 51.6 %copy-start.4 = (bf16[256,256]{1,0:T(8,128)(2,1)S(1)}, bf16[256,256]{1,0:T(8,128)(2,1)}, u32[]{:S(2)}) copy-start(bf16[256,256]{1,0:T(8,128)(2,1)} %col_out_ref.1) | copy-start | bytes 393220
  113.2 51.6 %copy-start.5 = (f32[256]{0:T(256)S(1)}, f32[256]{0:T(256)}, u32[]{:S(2)}) copy-start(f32[256]{0:T(256)} %param.23) | copy-start | bytes 3076
  113.2 51.6 %copy-start.6 = (f32[256]{0:T(256)S(1)}, f32[256]{0:T(256)}, u32[]{:S(2)}) copy-start(f32[256]{0:T(256)} %param.25) | copy-start | bytes 3076
  113.2 51.6 %copy-start.7 = (f32[256]{0:T(256)S(1)}, f32[256]{0:T(256)}, u32[]{:S(2)}) copy-start(f32[256]{0:T(256)} %param.27) | copy-start | bytes 3076
  113.3 51.6 %copy-start.8 = (f32[256]{0:T(256)S(1)}, f32[256]{0:T(256)}, u32[]{:S(2)}) copy-start(f32[256]{0:T(256)} %param.30) | copy-start | bytes 3076
  113.3 51.6 %copy-start.9 = (f32[256]{0:T(256)S(1)}, f32[256]{0:T(256)}, u32[]{:S(2)}) copy-start(f32[256]{0:T(256)} %param.32) | copy-start | bytes 3076
  113.3 51.6 %copy-start.10 = (f32[256]{0:T(256)S(1)}, f32[256]{0:T(256)}, u32[]{:S(2)}) copy-start(f32[256]{0:T(256)} %param.34) | copy-start | bytes 3076
  113.3 51.6 %copy-start.11 = (f32[256]{0:T(256)S(1)}, f32[256]{0:T(256)}, u32[]{:S(2)}) copy-start(f32[256]{0:T(256)} %param.35) | copy-start | bytes 3076
  113.3 1.2 copy-start.13
  114.6 1.0 copy-start.19
  140.0 24.8 %all-to-all-start.3 = ((bf16[64,40,128]{2,1,0:T(8,128)(2,1)}), bf16[64,40,128]{2,1,0:T(8,128)(2,1)S(1)}, u32[]{:S(2)}, u32[]{:S(2)}) async-start(bf16[64,40,128]{2,1,0:T(8,128)(2,1)} %bitcast.11), calls=%async_computation.3 | async-start | bytes 1310720 | tf_op jit(solution)/shard_map/all_to_all | solution.py:490
  164.9 1.0 copy-start.1
  165.9 1.0 copy-start.2
  (3 other events, 2.5 us)

commit v2 on v1

--- a/solution.py
+++ b/solution.py
@@ -47,11 +47,11 @@
 
 
 def pair_kernel(pair_ref, gain_ref, head_ref, bias_ref, project_ref, rows_ref):
-    channels, heads = head_ref.shape
+    heads, channels = head_ref.shape
 
     @pl.when(pl.program_id(0) == 0)
     def _():
-        gained = (gain_ref[...] * LOG2E) * head_ref[...].astype(F32).T
+        gained = (gain_ref[...] * LOG2E) * head_ref[...].astype(F32)
         gained = gained - jnp.mean(gained, axis=1, keepdims=True)
         high = gained.astype(BF16)
         low = (gained - high.astype(F32)).astype(BF16)
@@ -91,7 +91,7 @@
         in_specs=[
             pl.BlockSpec((parts * STEP, cols, channels), lambda i: (i, 0, 0)),
             pl.BlockSpec((1, channels), lambda i: (0, 0)),
-            pl.BlockSpec((channels, heads), lambda i: (0, 0)),
+            pl.BlockSpec((heads, channels), lambda i: (0, 0)),
         ],
         out_specs=pl.BlockSpec((heads, parts, STEP_ROWS, LANES), lambda i: (0, i, 0, 0)),
         out_shape=jax.ShapeDtypeStruct((heads, rows // STEP, STEP_ROWS, LANES), BF16),
@@ -101,7 +101,7 @@
         ],
         compiler_params=pltpu.CompilerParams(vmem_limit_bytes=VMEM),
         name="pair_bias",
-    )(coupled, gain[None], head_matrix)
+    )(coupled, gain[None], head_matrix.T)
 
 
 MASK_ROWS = 16

time: 196 us -> 194 us (0.990)
    unnamed x47 -> x46, local copies, waits for them, and re-layouts: 11.4 us -> 10 us
  transfers between devices with their start and end apart: 12 -> 12, of which waited for: 4 -> 4; matrix products, arithmetic and copies ran while one was open for 2% -> 2% of each run, Pallas kernels for 14% -> 15%
where the time goes in v2:
time: 194 us; the launch traced here: 193 us
  Pallas kernels  74.1 us (38%)
  waiting for transfers between devices  53.9 us (28%)
  starting transfers between devices  37.5 us (19%)
  blocking collectives  13.5 us (7%)
  local copies, waits for them, and re-layouts  13 us (7%)
    pallas_call x2, Pallas kernels, row_attention(): pl.pallas_call(functools.partial(row_kernel, turn=turn, count=count, resi...  47.5 us
    ppermute x2, waiting for transfers between devices, swap(): lax.ppermute(values, 'seq', [(r, (r + ring) % seq_size) for r in range(se...  18.9 us
    ppermute x5, waiting for transfers between devices, around(): lax.ppermute(values, 'seq', [(h * ring + z, h * ring + (z + by) % ring) f...  15.2 us
    all_to_all x1, blocking collectives, shards(): updated = lax.all_to_all(updated, 'seq', 0, 0)  13.5 us
    pallas_call x1, Pallas kernels, column_phase(): pl.pallas_call(functools.partial(column_kernel, heads=heads, scale=scale)...  13.4 us
    all_to_all x1, waiting for transfers between devices, shards(): lax.all_to_all(mixed, ('seq', 'res'), 0, 0, axis_index_groups=parity_all)  13 us
    all_to_all x1, starting transfers between devices, shards(): lax.all_to_all(mixed, ('seq', 'res'), 0, 0, axis_index_groups=parity_all)  10.8 us
    unnamed x46, local copies, waits for them, and re-layouts  10 us
  transfers between devices with their start and end apart: 12, of which 4 were waited for; matrix products, arithmetic and copies ran while one was open for 2% of the time, Pallas kernels for 15%

profile of v2, /device:TPU:0, one launch (start us, length us, event | category | flops | bytes accessed | tf_op | source)
XLA Modules:
  0.0 193.4 jit_solution(8853098298612421860)
XLA Ops:
  0.0 8.1 %pair_bias.1 = bf16[8,10,40,128]{3,2,1,0:T(8,128)(2,1)} custom-call(bf16[320,160,128]{2,1,0:T(8,128)(2,1)} %pair_ref.1, f32[1,128]{1,0:T(1,128)} %bitcast.48, bf16[8,128]{1,0:T(8,128)(2,1)} %bitcast.47), custom_call_target="tpu_custom_call" | custom-call | tf_op jit(solution)/shard_map/pair_bias/pallas_call | solution.py:88
  8.1 5.6 %all-to-all-start = ((bf16[16,5,40,128]{3,2,1,0:T(8,128)(2,1)}), bf16[16,5,40,128]{3,2,1,0:T(8,128)(2,1)S(1)}, u32[]{:S(2)}, u32[]{:S(2)}) async-start(bf16[16,5,40,128]{3,2,1,0:T(8,128)(2,1)} %bitcast.42), calls=%async_computation | async-start | bytes 1638400 | tf_op jit(solution)/shard_map/all_to_all | solution.py:451
  14.9 5.1 %pack_heads.1 = bf16[8,2,496,128]{3,2,1,0:T(8,128)(2,1)} custom-call(bf16[8,160,256]{2,1,0:T(8,128)(2,1)} %table_ref, bf16[2,16,128]{2,1,0:T(8,128)(2,1)} %bitcast_bitcast_fusion.mask_ref, f32[1,256]{1,0:T(1,128)} %bitcast.34, bf16[256,1024]{1,0:T(8,128)(2,1)} %weight_ref.1), custom_call_target="tpu_custom_call" | custom-call | tf_op jit(solution)/shard_map/pack_heads/pallas_call | solution.py:141
  20.1 1.0 pad_maximum_fusion
  21.1 6.7 %all-to-all-done.rest_0_ = bf16[16,5,40,128]{3,2,1,0:T(8,128)(2,1)S(1)} async-done(((bf16[16,5,40,128]{3,2,1,0:T(8,128)(2,1)}), bf16[16,5,40,128]{3,2,1,0:T(8,128)(2,1)S(1)}, u32[]{:S(2)}, u32[]{:S(2)}) %all-to-all-start) | async-done | bytes 819232 | tf_op jit(solution)/shard_map/all_to_all | solution.py:451
  27.8 3.6 %all-to-all-start.1 = ((bf16[8,2,496,128]{3,2,1,0:T(8,128)(2,1)}), bf16[8,2,496,128]{3,2,1,0:T(8,128)(2,1)S(1)}, u32[]{:S(2)}, u32[]{:S(2)}) async-start(bf16[8,2,496,128]{3,2,1,0:T(8,128)(2,1)} %pack_heads.1), calls=%async_computation.1 | async-start | bytes 4063232 | tf_op jit(solution)/shard_map/all_to_all | solution.py:466
  31.4 2.0 %collective-permute-start = (bf16[16,5,40,128]{3,2,1,0:T(8,128)(2,1)S(1)}, bf16[16,5,40,128]{3,2,1,0:T(8,128)(2,1)S(1)}, u32[]{:S(2)}, u32[]{:S(2)}) collective-permute-start(bf16[16,5,40,128]{3,2,1,0:T(8,128)(2,1)S(1)} %all-to-all-done.rest_0_), channel_id=1, source_target_pairs={{0,16},{16,32},{32,48},{48,0},{64,80},{80,96},{96,112},{112,64},{1... | collective-permute-start | bytes 2457608 | tf_op jit(solution)/shard_map/ppermute | solution.py:471
  33.4 2.2 %collective-permute-start.1 = (bf16[16,5,40,128]{3,2,1,0:T(8,128)(2,1)S(1)}, bf16[16,5,40,128]{3,2,1,0:T(8,128)(2,1)S(1)}, u32[]{:S(2)}, u32[]{:S(2)}) collective-permute-start(bf16[16,5,40,128]{3,2,1,0:T(8,128)(2,1)S(1)} %all-to-all-done.rest_0_), channel_id=1, source_target_pairs={{0,48},{16,0},{32,16},{48,32},{64,112},{80,64},{96,80},{112,96},{1... | collective-permute-start | bytes 2457608 | tf_op jit(solution)/shard_map/ppermute | solution.py:471
  35.6 2.9 %collective-permute-start.2 = (bf16[16,5,40,128]{3,2,1,0:T(8,128)(2,1)S(1)}, bf16[16,5,40,128]{3,2,1,0:T(8,128)(2,1)S(1)}, u32[]{:S(2)}, u32[]{:S(2)}) collective-permute-start(bf16[16,5,40,128]{3,2,1,0:T(8,128)(2,1)S(1)} %all-to-all-done.rest_0_), channel_id=1, source_target_pairs={{0,64},{16,80},{32,96},{48,112},{64,0},{80,16},{96,32},{112,48},{1... | collective-permute-start | bytes 2457608 | tf_op jit(solution)/shard_map/ppermute | solution.py:476
  38.5 15.2 %collective-permute-done.rest_1_ = bf16[16,5,40,128]{3,2,1,0:T(8,128)(2,1)S(1)} collective-permute-done((bf16[16,5,40,128]{3,2,1,0:T(8,128)(2,1)S(1)}, bf16[16,5,40,128]{3,2,1,0:T(8,128)(2,1)S(1)}, u32[]{:S(2)}, u32[]{:S(2)}) %collective-permute-start) | collective-permute-done | bytes 819232 | tf_op jit(solution)/shard_map/ppermute | solution.py:471
  53.7 0.9 copy-done.14
  54.6 0.9 copy-done.16
  55.5 18.9 %collective-permute-done.2.rest_0_ = bf16[16,5,40,128]{3,2,1,0:T(8,128)(2,1)S(1)} collective-permute-done((bf16[16,5,40,128]{3,2,1,0:T(8,128)(2,1)S(1)}, bf16[16,5,40,128]{3,2,1,0:T(8,128)(2,1)S(1)}, u32[]{:S(2)}, u32[]{:S(2)}) %collective-permute-start.2) | collective-permute-done | bytes 819232 | tf_op jit(solution)/shard_map/ppermute | solution.py:476
  74.5 0.9 copy-done.12
  75.4 2.0 %collective-permute-start.5 = (bf16[16,5,40,128]{3,2,1,0:T(8,128)(2,1)}, bf16[16,5,40,128]{3,2,1,0:T(8,128)(2,1)}, u32[]{:S(2)}, u32[]{:S(2)}) collective-permute-start(bf16[16,5,40,128]{3,2,1,0:T(8,128)(2,1)} %copy-done.12), channel_id=1, source_target_pairs={{0,16},{16,32},{32,48},{48,0},{64,80},{80,96},{96,112},{112,64},{1... | collective-permute-start | bytes 2457608 | tf_op jit(solution)/shard_map/ppermute | solution.py:471
  77.4 2.2 %collective-permute-start.6 = (bf16[16,5,40,128]{3,2,1,0:T(8,128)(2,1)}, bf16[16,5,40,128]{3,2,1,0:T(8,128)(2,1)}, u32[]{:S(2)}, u32[]{:S(2)}) collective-permute-start(bf16[16,5,40,128]{3,2,1,0:T(8,128)(2,1)} %copy-done.12), channel_id=1, source_target_pairs={{0,48},{16,0},{32,16},{48,32},{64,112},{80,64},{96,80},{112,96},{1... | collective-permute-start | bytes 2457608 | tf_op jit(solution)/shard_map/ppermute | solution.py:471
  79.6 0.9 collective-permute-start.7
  80.5 5.2 %all-to-all-start.2 = ((bf16[8,21,8,256]{3,2,1,0:T(8,128)(2,1)}), bf16[8,21,8,256]{3,2,1,0:T(8,128)(2,1)S(1)}, u32[]{:S(2)}, u32[]{:S(2)}) async-start(bf16[8,21,8,256]{3,2,1,0:T(8,128)(2,1)} %pad_maximum_fusion), calls=%async_computation.2 | async-start | bytes 1376256 | tf_op jit(solution)/shard_map/all_to_all | solution.py:486
  85.8 1.1 copy-done.15
  86.9 1.1 copy-done.17
  88.1 23.0 %row_attention.2.rest_4_ = bf16[8,4,40,128]{3,2,1,0:T(8,128)(2,1)S(1)} custom-call(s32[3]{0:T(128)S(1)} %pad_add_fusion.place_ref, bf16[8,2,496,128]{3,2,1,0:T(8,128)(2,1)S(1)} %all-to-all-done.1.own_ref, bf16[8,2,496,128]{3,2,1,0:T(8,128)(2,1)} %collective-permute-done.4.other_ref, bf16[16,5,40,128]{3,2,1,0:T(8,128)(2,1)S(1)} %all-to-all-done.rest_0_, ...), custom_call_target="tpu_custom_call" | custom-call | flops 6710886400 | bytes 12000000 | tf_op jit(solution)/shard_map/row_attention/pallas_call | solution.py:291
  111.9 1.2 copy-done.13
  113.1 1.0 copy-done.19
  114.1 24.5 %row_attention.3 = bf16[8,8,40,128]{3,2,1,0:T(8,128)(2,1)} custom-call(s32[3]{0:T(128)S(1)} %pad_add_fusion.place_ref, bf16[8,2,496,128]{3,2,1,0:T(8,128)(2,1)S(1)} %all-to-all-done.1.own_ref, bf16[8,2,496,128]{3,2,1,0:T(8,128)(2,1)} %collective-permute-done.4.other_ref, bf16[16,5,40,128]{3,2,1,0:T(8,128)(2,1)S(1)} %copy-done.13, ...), custom_call_target="tpu_custom_call" | custom-call | flops 6710886400 | bytes 12000000 | tf_op jit(solution)/shard_map/row_attention/pallas_call | solution.py:291
  138.6 10.8 %all-to-all-start.3 = ((bf16[64,40,128]{2,1,0:T(8,128)(2,1)}), bf16[64,40,128]{2,1,0:T(8,128)(2,1)S(1)}, u32[]{:S(2)}, u32[]{:S(2)}) async-start(bf16[64,40,128]{2,1,0:T(8,128)(2,1)} %bitcast.12), calls=%async_computation.3 | async-start | bytes 1310720 | tf_op jit(solution)/shard_map/all_to_all | solution.py:490
  149.4 0.9 slice.3.row_gate_ref
  150.3 13.0 %all-to-all-done.3 = bf16[64,40,128]{2,1,0:T(8,128)(2,1)S(1)} async-done(((bf16[64,40,128]{2,1,0:T(8,128)(2,1)}), bf16[64,40,128]{2,1,0:T(8,128)(2,1)S(1)}, u32[]{:S(2)}, u32[]{:S(2)}) %all-to-all-start.3) | async-done | bytes 655392 | tf_op jit(solution)/shard_map/all_to_all | solution.py:490
  163.5 1.0 copy-done.1
  164.5 1.0 copy-done.2
  165.5 13.4 %column_phase.1 = bf16[8,20,8,256]{3,2,1,0:T(8,128)(2,1)S(1)} custom-call(bf16[8,8,40,128]{3,2,1,0:T(8,128)(2,1)S(1)} %bitcast.33, bf16[8,21,8,256]{3,2,1,0:T(8,128)(2,1)S(1)} %all-to-all-done.2.table_ref.mask_ref, bf16[8,21,8,256]{3,2,1,0:T(8,128)(2,1)S(1)} %all-to-all-done.2.table_ref.mask_ref, f32[1,256]{1,0:T(1,128)S(1)} %bitcast.35, ...), custom_call_target="tpu_custom_call" | custom-call | tf_op jit(solution)/shard_map/column_phase/pallas_call | solution.py:404
  179.0 13.5 %all_to_all.25 = bf16[8,20,8,256]{3,2,1,0:T(8,128)(2,1)S(1)} all-to-all(bf16[8,20,8,256]{3,2,1,0:T(8,128)(2,1)S(1)} %column_phase.1), channel_id=1, replica_groups=mesh['seq'=8,'res'=16] {'seq'}, dimensions={0} | all-to-all | bytes 1310720 | tf_op jit(solution)/shard_map/all_to_all | solution.py:509
  192.5 1.0 copy.30
  (55 shorter events, 2.0 us)
Async XLA Ops:
  8.1 5.7 %copy-start.20 = (bf16[8,160,256]{2,1,0:T(8,128)(2,1)S(1)}, bf16[8,160,256]{2,1,0:T(8,128)(2,1)}, u32[]{:S(2)}) copy-start(bf16[8,160,256]{2,1,0:T(8,128)(2,1)} %table_ref) | copy-start | bytes 1966084
  8.1 6.1 %copy-start.21 = (s32[8,160]{1,0:T(8,128)S(1)}, s32[8,160]{1,0:T(8,128)}, u32[]{:S(2)}) copy-start(s32[8,160]{1,0:T(8,128)} %param.21) | copy-start | bytes 15364
  8.1 6.2 %copy-start.22 = (s32[160]{0:T(256)S(1)}, s32[160]{0:T(256)}, u32[]{:S(2)}) copy-start(s32[160]{0:T(256)} %param.22) | copy-start | bytes 1924
  8.1 19.7 %all-to-all-start = ((bf16[16,5,40,128]{3,2,1,0:T(8,128)(2,1)}), bf16[16,5,40,128]{3,2,1,0:T(8,128)(2,1)S(1)}, u32[]{:S(2)}, u32[]{:S(2)}) async-start(bf16[16,5,40,128]{3,2,1,0:T(8,128)(2,1)} %bitcast.42), calls=%async_computation | async-start | bytes 1638400 | tf_op jit(solution)/shard_map/all_to_all | solution.py:451
  27.8 47.6 %all-to-all-start.1 = ((bf16[8,2,496,128]{3,2,1,0:T(8,128)(2,1)}), bf16[8,2,496,128]{3,2,1,0:T(8,128)(2,1)S(1)}, u32[]{:S(2)}, u32[]{:S(2)}) async-start(bf16[8,2,496,128]{3,2,1,0:T(8,128)(2,1)} %pack_heads.1), calls=%async_computation.1 | async-start | bytes 4063232 | tf_op jit(solution)/shard_map/all_to_all | solution.py:466
  31.4 22.3 %collective-permute-start = (bf16[16,5,40,128]{3,2,1,0:T(8,128)(2,1)S(1)}, bf16[16,5,40,128]{3,2,1,0:T(8,128)(2,1)S(1)}, u32[]{:S(2)}, u32[]{:S(2)}) collective-permute-start(bf16[16,5,40,128]{3,2,1,0:T(8,128)(2,1)S(1)} %all-to-all-done.rest_0_), channel_id=1, source_target_pairs={{0,16},{16,32},{32,48},{48,0},{64,80},{80,96},{96,112},{112,64},{1... | collective-permute-start | bytes 2457608 | tf_op jit(solution)/shard_map/ppermute | solution.py:471
  33.4 21.2 %collective-permute-start.1 = (bf16[16,5,40,128]{3,2,1,0:T(8,128)(2,1)S(1)}, bf16[16,5,40,128]{3,2,1,0:T(8,128)(2,1)S(1)}, u32[]{:S(2)}, u32[]{:S(2)}) collective-permute-start(bf16[16,5,40,128]{3,2,1,0:T(8,128)(2,1)S(1)} %all-to-all-done.rest_0_), channel_id=1, source_target_pairs={{0,48},{16,0},{32,16},{48,32},{64,112},{80,64},{96,80},{112,96},{1... | collective-permute-start | bytes 2457608 | tf_op jit(solution)/shard_map/ppermute | solution.py:471
  35.6 38.9 %collective-permute-start.2 = (bf16[16,5,40,128]{3,2,1,0:T(8,128)(2,1)S(1)}, bf16[16,5,40,128]{3,2,1,0:T(8,128)(2,1)S(1)}, u32[]{:S(2)}, u32[]{:S(2)}) collective-permute-start(bf16[16,5,40,128]{3,2,1,0:T(8,128)(2,1)S(1)} %all-to-all-done.rest_0_), channel_id=1, source_target_pairs={{0,64},{16,80},{32,96},{48,112},{64,0},{80,16},{96,32},{112,48},{1... | collective-permute-start | bytes 2457608 | tf_op jit(solution)/shard_map/ppermute | solution.py:476
  53.7 21.7 %collective-permute-start.3 = (bf16[16,5,40,128]{3,2,1,0:T(8,128)(2,1)S(1)}, bf16[16,5,40,128]{3,2,1,0:T(8,128)(2,1)}, u32[]{:S(2)}, u32[]{:S(2)}) collective-permute-start(bf16[16,5,40,128]{3,2,1,0:T(8,128)(2,1)S(1)} %collective-permute-done.rest_1_), channel_id=1, source_target_pairs={{0,16},{16,32},{32,48},{48,0},{64,80},{80,96},{96,112},{112,64},{1... | collective-permute-start | bytes 2457608 | tf_op jit(solution)/shard_map/ppermute | solution.py:471
  74.5 0.9 copy-start.12
  75.4 10.4 %collective-permute-start.4 = (bf16[8,2,496,128]{3,2,1,0:T(8,128)(2,1)S(1)}, bf16[8,2,496,128]{3,2,1,0:T(8,128)(2,1)}, u32[]{:S(2)}, u32[]{:S(2)}) collective-permute-start(bf16[8,2,496,128]{3,2,1,0:T(8,128)(2,1)S(1)} %all-to-all-done.1.own_ref), channel_id=1, source_target_pairs={{0,1},{1,0},{2,3},{3,2},{4,5},{5,4},{6,7},{7,6},{8,9},{9,8},{10,11... | collective-permute-start | bytes 6094856 | tf_op jit(solution)/shard_map/ppermute | solution.py:481
  75.4 36.5 %collective-permute-start.5 = (bf16[16,5,40,128]{3,2,1,0:T(8,128)(2,1)}, bf16[16,5,40,128]{3,2,1,0:T(8,128)(2,1)}, u32[]{:S(2)}, u32[]{:S(2)}) collective-permute-start(bf16[16,5,40,128]{3,2,1,0:T(8,128)(2,1)} %copy-done.12), channel_id=1, source_target_pairs={{0,16},{16,32},{32,48},{48,0},{64,80},{80,96},{96,112},{112,64},{1... | collective-permute-start | bytes 2457608 | tf_op jit(solution)/shard_map/ppermute | solution.py:471
  77.4 34.5 %collective-permute-start.6 = (bf16[16,5,40,128]{3,2,1,0:T(8,128)(2,1)}, bf16[16,5,40,128]{3,2,1,0:T(8,128)(2,1)}, u32[]{:S(2)}, u32[]{:S(2)}) collective-permute-start(bf16[16,5,40,128]{3,2,1,0:T(8,128)(2,1)} %copy-done.12), channel_id=1, source_target_pairs={{0,48},{16,0},{32,16},{48,32},{64,112},{80,64},{96,80},{112,96},{1... | collective-permute-start | bytes 2457608 | tf_op jit(solution)/shard_map/ppermute | solution.py:471
  79.6 32.3 %collective-permute-start.7 = (bf16[16,5,40,128]{3,2,1,0:T(8,128)(2,1)}, bf16[16,5,40,128]{3,2,1,0:T(8,128)(2,1)}, u32[]{:S(2)}, u32[]{:S(2)}) collective-permute-start(bf16[16,5,40,128]{3,2,1,0:T(8,128)(2,1)} %collective-permute-done.3.rest_3_), channel_id=1, source_target_pairs={{0,64},{16,80},{32,96},{48,112},{64,0},{80,16},{96,32},{112,48},{1... | collective-permute-start | bytes 2457608 | tf_op jit(solution)/shard_map/ppermute | solution.py:476
  80.5 31.3 %all-to-all-start.2 = ((bf16[8,21,8,256]{3,2,1,0:T(8,128)(2,1)}), bf16[8,21,8,256]{3,2,1,0:T(8,128)(2,1)S(1)}, u32[]{:S(2)}, u32[]{:S(2)}) async-start(bf16[8,21,8,256]{3,2,1,0:T(8,128)(2,1)} %pad_maximum_fusion), calls=%async_computation.2 | async-start | bytes 1376256 | tf_op jit(solution)/shard_map/all_to_all | solution.py:486
  85.8 1.1 copy-start.15
  86.9 1.1 copy-start.17
  111.8 51.6 %copy-start = (bf16[256,1024]{1,0:T(8,128)(2,1)S(1)}, bf16[256,1024]{1,0:T(8,128)(2,1)}, u32[]{:S(2)}) copy-start(bf16[256,1024]{1,0:T(8,128)(2,1)} %col_weight_ref.1) | copy-start | bytes 1572868
  111.8 51.6 %copy-start.3 = (bf16[256,256]{1,0:T(8,128)(2,1)S(1)}, bf16[256,256]{1,0:T(8,128)(2,1)}, u32[]{:S(2)}) copy-start(bf16[256,256]{1,0:T(8,128)(2,1)} %row_out_ref.1) | copy-start | bytes 393220
  111.8 51.6 %copy-start.4 = (bf16[256,256]{1,0:T(8,128)(2,1)S(1)}, bf16[256,256]{1,0:T(8,128)(2,1)}, u32[]{:S(2)}) copy-start(bf16[256,256]{1,0:T(8,128)(2,1)} %col_out_ref.1) | copy-start | bytes 393220
  111.8 51.6 %copy-start.5 = (f32[256]{0:T(256)S(1)}, f32[256]{0:T(256)}, u32[]{:S(2)}) copy-start(f32[256]{0:T(256)} %param.23) | copy-start | bytes 3076
  111.8 51.6 %copy-start.6 = (f32[256]{0:T(256)S(1)}, f32[256]{0:T(256)}, u32[]{:S(2)}) copy-start(f32[256]{0:T(256)} %param.25) | copy-start | bytes 3076
  111.8 51.6 %copy-start.7 = (f32[256]{0:T(256)S(1)}, f32[256]{0:T(256)}, u32[]{:S(2)}) copy-start(f32[256]{0:T(256)} %param.27) | copy-start | bytes 3076
  111.8 51.6 %copy-start.8 = (f32[256]{0:T(256)S(1)}, f32[256]{0:T(256)}, u32[]{:S(2)}) copy-start(f32[256]{0:T(256)} %param.30) | copy-start | bytes 3076
  111.8 51.6 %copy-start.9 = (f32[256]{0:T(256)S(1)}, f32[256]{0:T(256)}, u32[]{:S(2)}) copy-start(f32[256]{0:T(256)} %param.32) | copy-start | bytes 3076
  111.8 51.6 %copy-start.10 = (f32[256]{0:T(256)S(1)}, f32[256]{0:T(256)}, u32[]{:S(2)}) copy-start(f32[256]{0:T(256)} %param.34) | copy-start | bytes 3076
  111.8 51.6 %copy-start.11 = (f32[256]{0:T(256)S(1)}, f32[256]{0:T(256)}, u32[]{:S(2)}) copy-start(f32[256]{0:T(256)} %param.35) | copy-start | bytes 3076
  111.9 1.2 copy-start.13
  113.1 1.0 copy-start.19
  138.6 24.8 %all-to-all-start.3 = ((bf16[64,40,128]{2,1,0:T(8,128)(2,1)}), bf16[64,40,128]{2,1,0:T(8,128)(2,1)S(1)}, u32[]{:S(2)}, u32[]{:S(2)}) async-start(bf16[64,40,128]{2,1,0:T(8,128)(2,1)} %bitcast.12), calls=%async_computation.3 | async-start | bytes 1310720 | tf_op jit(solution)/shard_map/all_to_all | solution.py:490
  163.4 1.0 copy-start.1
  164.5 1.0 copy-start.2
  (3 other events, 2.5 us)

commit v3 on v2

--- a/solution.py
+++ b/solution.py
@@ -170,6 +170,10 @@
     main = 2 * blocks * LANES
     core = place_ref[0]
     there = (place_ref[1] + turn) % 2 * count
+
+    def place_of(number):
+        return there + (place_ref[2] + (0, -1, 1, 2)[number] + count) % count
+
     lane8 = lanes_of((EIGHT, LANES))
     lane = lanes_of((residues, LANES))
 
@@ -233,38 +237,42 @@
                         value_ref[s, head_at : head_at + LANES] = kept[:LANES]
                         value_ref[s, tail_at : tail_at + STEP] = kept[LANES:]
 
+    def place_at(block):
+        place = place_of(0)
+        for number in range(1, count):
+            place = jnp.where(block == number, place_of(number), place)
+        return place
+
+    def query_of(block, s):
+        member = s % group
+        spare = (member + 1) % group * head_size + s
+        inside = (lane >= member * head_size) & (lane < (member + 1) * head_size)
+        raw = own_ref[place_at(block), s // group, :residues, :].astype(F32)
+        return jnp.where(inside, raw, jnp.where(lane == spare, 1.0, 0.0)).astype(BF16)
+
+    def score(block, s, query, j):
+        columns = slice(j * chunk, (j + 1) * chunk)
+        score_ref[s % 2, :, columns] = dot_nt(query, key_ref[s, columns, :]) + bias32_ref[block, :, columns]
+
     def body(block, carry):
-        ahead = jnp.where(block == 1, -1, jnp.where(block == 2, 1, jnp.where(block == 3, 2, 0)))
-        place = there + (place_ref[2] + ahead + count) % count
-
-        def query_of(s):
-            member = s % group
-            spare = (member + 1) % group * head_size + s
-            inside = (lane >= member * head_size) & (lane < (member + 1) * head_size)
-            raw = own_ref[place, s // group, :residues, :].astype(F32)
-            return jnp.where(inside, raw, jnp.where(lane == spare, 1.0, 0.0)).astype(BF16)
-
-        def score(s, query, j):
-            columns = slice(j * chunk, (j + 1) * chunk)
-            score_ref[s % 2, :, columns] = dot_nt(query, key_ref[s, columns, :]) + bias32_ref[block, :, columns]
+        place = place_at(block)
+        target = place if earlier else block
+        following = jnp.minimum(block + 1, count - 1)
 
         def weigh(s, row):
             scores = score_ref[s % 2, row : row + TILE, :]
             top = jnp.max(scores, axis=1, keepdims=True)
             weight_ref[s % 2, row : row + TILE, :] = jnp.exp2(scores - top).astype(BF16)
 
-        query = query_of(0)
-        for j in range(keys // chunk):
-            score(0, query, j)
         total = None
         for s in range(lines):
             member, pack = s % group, s // group
-            query = query_of(s + 1) if s + 1 < lines else None
+            ahead = (block, s + 1) if s + 1 < lines else (following, 0)
+            query = query_of(*ahead)
             steps = keys // chunk
             tiles = residues // TILE
             for j in range(steps):
-                if query is not None:
-                    score(s + 1, query, j)
+                score(*ahead, query, j)
                 for r in range(j * tiles // steps, (j + 1) * tiles // steps):
                     weigh(s, r * TILE)
             mixed = dot(weight_ref[s % 2], value_ref[s])
@@ -277,6 +285,9 @@
                     out_ref[piece, place % targets, pack * span : (pack + 1) * span, :] = part
         return carry
 
+    query = query_of(0, 0)
+    for j in range(keys // chunk):
+        score(0, 0, query, j)
     lax.fori_loop(0, count, body, 0)
 
 
@@ -376,7 +387,7 @@
         scores = jnp.where(present[None] > 0, scores, -1e9)
         top = jnp.max(scores, axis=1, keepdims=True)
         weights = jnp.exp2(scores - top)
-        weights = weights / jnp.sum(weights, axis=1, keepdims=True)
+        weights = weights * (1.0 / jnp.sum(weights, axis=1, keepdims=True))
         weights = weights.astype(BF16).reshape(heads * rows, rows)
         attended.append(dot_tn(weights, spread_value))
     gated = (jnp.concatenate(attended, axis=0) * gate).astype(BF16)

time: 194 us -> 194 us (level)
  transfers between devices with their start and end apart: 12 -> 12, of which waited for: 4 -> 4; matrix products, arithmetic and copies ran while one was open for 2% -> 2% of each run, Pallas kernels for 15% -> 14%
where the time goes in v3:
time: 194 us; the launch traced here: 193 us
  Pallas kernels  74 us (38%)
  waiting for transfers between devices  53.9 us (28%)
  starting transfers between devices  37.5 us (19%)
  blocking collectives  13.5 us (7%)
  local copies, waits for them, and re-layouts  13 us (7%)
    pallas_call x2, Pallas kernels, row_attention(): pl.pallas_call(functools.partial(row_kernel, turn=turn, count=count, resi...  47.4 us
    ppermute x2, waiting for transfers between devices, swap(): lax.ppermute(values, 'seq', [(r, (r + ring) % seq_size) for r in range(se...  18.9 us
    ppermute x5, waiting for transfers between devices, around(): lax.ppermute(values, 'seq', [(h * ring + z, h * ring + (z + by) % ring) f...  15.2 us
    all_to_all x1, blocking collectives, shards(): updated = lax.all_to_all(updated, 'seq', 0, 0)  13.5 us
    pallas_call x1, Pallas kernels, column_phase(): pl.pallas_call(functools.partial(column_kernel, heads=heads, scale=scale)...  13.4 us
    all_to_all x1, waiting for transfers between devices, shards(): lax.all_to_all(mixed, ('seq', 'res'), 0, 0, axis_index_groups=parity_all)  13 us
    all_to_all x1, starting transfers between devices, shards(): lax.all_to_all(mixed, ('seq', 'res'), 0, 0, axis_index_groups=parity_all)  10.8 us
    unnamed x46, local copies, waits for them, and re-layouts  10 us
  transfers between devices with their start and end apart: 12, of which 4 were waited for; matrix products, arithmetic and copies ran while one was open for 2% of the time, Pallas kernels for 14%

profile of v3, /device:TPU:0, one launch (start us, length us, event | category | flops | bytes accessed | tf_op | source)
XLA Modules:
  0.0 193.3 jit_solution(1575100232878578692)
XLA Ops:
  0.0 8.1 %pair_bias.1 = bf16[8,10,40,128]{3,2,1,0:T(8,128)(2,1)} custom-call(bf16[320,160,128]{2,1,0:T(8,128)(2,1)} %pair_ref.1, f32[1,128]{1,0:T(1,128)} %bitcast.48, bf16[8,128]{1,0:T(8,128)(2,1)} %bitcast.47), custom_call_target="tpu_custom_call" | custom-call | tf_op jit(solution)/shard_map/pair_bias/pallas_call | solution.py:88
  8.1 5.6 %all-to-all-start = ((bf16[16,5,40,128]{3,2,1,0:T(8,128)(2,1)}), bf16[16,5,40,128]{3,2,1,0:T(8,128)(2,1)S(1)}, u32[]{:S(2)}, u32[]{:S(2)}) async-start(bf16[16,5,40,128]{3,2,1,0:T(8,128)(2,1)} %bitcast.42), calls=%async_computation | async-start | bytes 1638400 | tf_op jit(solution)/shard_map/all_to_all | solution.py:462
  14.9 5.1 %pack_heads.1 = bf16[8,2,496,128]{3,2,1,0:T(8,128)(2,1)} custom-call(bf16[8,160,256]{2,1,0:T(8,128)(2,1)} %table_ref, bf16[2,16,128]{2,1,0:T(8,128)(2,1)} %bitcast_bitcast_fusion.mask_ref, f32[1,256]{1,0:T(1,128)} %bitcast.34, bf16[256,1024]{1,0:T(8,128)(2,1)} %weight_ref.1), custom_call_target="tpu_custom_call" | custom-call | tf_op jit(solution)/shard_map/pack_heads/pallas_call | solution.py:141
  20.1 1.0 pad_maximum_fusion
  21.1 6.7 %all-to-all-done.rest_0_ = bf16[16,5,40,128]{3,2,1,0:T(8,128)(2,1)S(1)} async-done(((bf16[16,5,40,128]{3,2,1,0:T(8,128)(2,1)}), bf16[16,5,40,128]{3,2,1,0:T(8,128)(2,1)S(1)}, u32[]{:S(2)}, u32[]{:S(2)}) %all-to-all-start) | async-done | bytes 819232 | tf_op jit(solution)/shard_map/all_to_all | solution.py:462
  27.8 3.6 %all-to-all-start.1 = ((bf16[8,2,496,128]{3,2,1,0:T(8,128)(2,1)}), bf16[8,2,496,128]{3,2,1,0:T(8,128)(2,1)S(1)}, u32[]{:S(2)}, u32[]{:S(2)}) async-start(bf16[8,2,496,128]{3,2,1,0:T(8,128)(2,1)} %pack_heads.1), calls=%async_computation.1 | async-start | bytes 4063232 | tf_op jit(solution)/shard_map/all_to_all | solution.py:477
  31.4 2.0 %collective-permute-start = (bf16[16,5,40,128]{3,2,1,0:T(8,128)(2,1)S(1)}, bf16[16,5,40,128]{3,2,1,0:T(8,128)(2,1)S(1)}, u32[]{:S(2)}, u32[]{:S(2)}) collective-permute-start(bf16[16,5,40,128]{3,2,1,0:T(8,128)(2,1)S(1)} %all-to-all-done.rest_0_), channel_id=1, source_target_pairs={{0,16},{16,32},{32,48},{48,0},{64,80},{80,96},{96,112},{112,64},{1... | collective-permute-start | bytes 2457608 | tf_op jit(solution)/shard_map/ppermute | solution.py:482
  33.4 2.2 %collective-permute-start.1 = (bf16[16,5,40,128]{3,2,1,0:T(8,128)(2,1)S(1)}, bf16[16,5,40,128]{3,2,1,0:T(8,128)(2,1)S(1)}, u32[]{:S(2)}, u32[]{:S(2)}) collective-permute-start(bf16[16,5,40,128]{3,2,1,0:T(8,128)(2,1)S(1)} %all-to-all-done.rest_0_), channel_id=1, source_target_pairs={{0,48},{16,0},{32,16},{48,32},{64,112},{80,64},{96,80},{112,96},{1... | collective-permute-start | bytes 2457608 | tf_op jit(solution)/shard_map/ppermute | solution.py:482
  35.6 2.9 %collective-permute-start.2 = (bf16[16,5,40,128]{3,2,1,0:T(8,128)(2,1)S(1)}, bf16[16,5,40,128]{3,2,1,0:T(8,128)(2,1)S(1)}, u32[]{:S(2)}, u32[]{:S(2)}) collective-permute-start(bf16[16,5,40,128]{3,2,1,0:T(8,128)(2,1)S(1)} %all-to-all-done.rest_0_), channel_id=1, source_target_pairs={{0,64},{16,80},{32,96},{48,112},{64,0},{80,16},{96,32},{112,48},{1... | collective-permute-start | bytes 2457608 | tf_op jit(solution)/shard_map/ppermute | solution.py:487
  38.5 15.2 %collective-permute-done.rest_1_ = bf16[16,5,40,128]{3,2,1,0:T(8,128)(2,1)S(1)} collective-permute-done((bf16[16,5,40,128]{3,2,1,0:T(8,128)(2,1)S(1)}, bf16[16,5,40,128]{3,2,1,0:T(8,128)(2,1)S(1)}, u32[]{:S(2)}, u32[]{:S(2)}) %collective-permute-start) | collective-permute-done | bytes 819232 | tf_op jit(solution)/shard_map/ppermute | solution.py:482
  53.7 0.9 copy-done.14
  54.6 0.9 copy-done.16
  55.5 18.9 %collective-permute-done.2.rest_0_ = bf16[16,5,40,128]{3,2,1,0:T(8,128)(2,1)S(1)} collective-permute-done((bf16[16,5,40,128]{3,2,1,0:T(8,128)(2,1)S(1)}, bf16[16,5,40,128]{3,2,1,0:T(8,128)(2,1)S(1)}, u32[]{:S(2)}, u32[]{:S(2)}) %collective-permute-start.2) | collective-permute-done | bytes 819232 | tf_op jit(solution)/shard_map/ppermute | solution.py:487
  74.5 0.9 copy-done.12
  75.4 2.0 %collective-permute-start.5 = (bf16[16,5,40,128]{3,2,1,0:T(8,128)(2,1)}, bf16[16,5,40,128]{3,2,1,0:T(8,128)(2,1)}, u32[]{:S(2)}, u32[]{:S(2)}) collective-permute-start(bf16[16,5,40,128]{3,2,1,0:T(8,128)(2,1)} %copy-done.12), channel_id=1, source_target_pairs={{0,16},{16,32},{32,48},{48,0},{64,80},{80,96},{96,112},{112,64},{1... | collective-permute-start | bytes 2457608 | tf_op jit(solution)/shard_map/ppermute | solution.py:482
  77.4 2.2 %collective-permute-start.6 = (bf16[16,5,40,128]{3,2,1,0:T(8,128)(2,1)}, bf16[16,5,40,128]{3,2,1,0:T(8,128)(2,1)}, u32[]{:S(2)}, u32[]{:S(2)}) collective-permute-start(bf16[16,5,40,128]{3,2,1,0:T(8,128)(2,1)} %copy-done.12), channel_id=1, source_target_pairs={{0,48},{16,0},{32,16},{48,32},{64,112},{80,64},{96,80},{112,96},{1... | collective-permute-start | bytes 2457608 | tf_op jit(solution)/shard_map/ppermute | solution.py:482
  79.6 0.9 collective-permute-start.7
  80.5 5.2 %all-to-all-start.2 = ((bf16[8,21,8,256]{3,2,1,0:T(8,128)(2,1)}), bf16[8,21,8,256]{3,2,1,0:T(8,128)(2,1)S(1)}, u32[]{:S(2)}, u32[]{:S(2)}) async-start(bf16[8,21,8,256]{3,2,1,0:T(8,128)(2,1)} %pad_maximum_fusion), calls=%async_computation.2 | async-start | bytes 1376256 | tf_op jit(solution)/shard_map/all_to_all | solution.py:497
  85.8 1.1 copy-done.15
  86.9 1.1 copy-done.17
  88.1 22.9 %row_attention.2.rest_4_ = bf16[8,4,40,128]{3,2,1,0:T(8,128)(2,1)S(1)} custom-call(s32[3]{0:T(128)S(1)} %pad_add_fusion.place_ref, bf16[8,2,496,128]{3,2,1,0:T(8,128)(2,1)S(1)} %all-to-all-done.1.own_ref, bf16[8,2,496,128]{3,2,1,0:T(8,128)(2,1)} %collective-permute-done.4.other_ref, bf16[16,5,40,128]{3,2,1,0:T(8,128)(2,1)S(1)} %all-to-all-done.rest_0_, ...), custom_call_target="tpu_custom_call" | custom-call | flops 6710886400 | bytes 12000000 | tf_op jit(solution)/shard_map/row_attention/pallas_call | solution.py:302
  111.8 1.2 copy-done.13
  113.0 1.0 copy-done.19
  114.0 24.5 %row_attention.3 = bf16[8,8,40,128]{3,2,1,0:T(8,128)(2,1)} custom-call(s32[3]{0:T(128)S(1)} %pad_add_fusion.place_ref, bf16[8,2,496,128]{3,2,1,0:T(8,128)(2,1)S(1)} %all-to-all-done.1.own_ref, bf16[8,2,496,128]{3,2,1,0:T(8,128)(2,1)} %collective-permute-done.4.other_ref, bf16[16,5,40,128]{3,2,1,0:T(8,128)(2,1)S(1)} %copy-done.13, ...), custom_call_target="tpu_custom_call" | custom-call | flops 6710886400 | bytes 12000000 | tf_op jit(solution)/shard_map/row_attention/pallas_call | solution.py:302
  138.5 10.8 %all-to-all-start.3 = ((bf16[64,40,128]{2,1,0:T(8,128)(2,1)}), bf16[64,40,128]{2,1,0:T(8,128)(2,1)S(1)}, u32[]{:S(2)}, u32[]{:S(2)}) async-start(bf16[64,40,128]{2,1,0:T(8,128)(2,1)} %bitcast.12), calls=%async_computation.3 | async-start | bytes 1310720 | tf_op jit(solution)/shard_map/all_to_all | solution.py:501
  149.3 0.9 slice.3.row_gate_ref
  150.2 13.0 %all-to-all-done.3 = bf16[64,40,128]{2,1,0:T(8,128)(2,1)S(1)} async-done(((bf16[64,40,128]{2,1,0:T(8,128)(2,1)}), bf16[64,40,128]{2,1,0:T(8,128)(2,1)S(1)}, u32[]{:S(2)}, u32[]{:S(2)}) %all-to-all-start.3) | async-done | bytes 655392 | tf_op jit(solution)/shard_map/all_to_all | solution.py:501
  163.4 1.0 copy-done.1
  164.4 1.0 copy-done.2
  165.4 13.4 %column_phase.1 = bf16[8,20,8,256]{3,2,1,0:T(8,128)(2,1)S(1)} custom-call(bf16[8,8,40,128]{3,2,1,0:T(8,128)(2,1)S(1)} %bitcast.33, bf16[8,21,8,256]{3,2,1,0:T(8,128)(2,1)S(1)} %all-to-all-done.2.table_ref.mask_ref, bf16[8,21,8,256]{3,2,1,0:T(8,128)(2,1)S(1)} %all-to-all-done.2.table_ref.mask_ref, f32[1,256]{1,0:T(1,128)S(1)} %bitcast.35, ...), custom_call_target="tpu_custom_call" | custom-call | tf_op jit(solution)/shard_map/column_phase/pallas_call | solution.py:415
  178.9 13.5 %all_to_all.25 = bf16[8,20,8,256]{3,2,1,0:T(8,128)(2,1)S(1)} all-to-all(bf16[8,20,8,256]{3,2,1,0:T(8,128)(2,1)S(1)} %column_phase.1), channel_id=1, replica_groups=mesh['seq'=8,'res'=16] {'seq'}, dimensions={0} | all-to-all | bytes 1310720 | tf_op jit(solution)/shard_map/all_to_all | solution.py:520
  192.3 1.0 copy.30
  (55 shorter events, 2.0 us)
Async XLA Ops:
  8.1 5.7 %copy-start.20 = (bf16[8,160,256]{2,1,0:T(8,128)(2,1)S(1)}, bf16[8,160,256]{2,1,0:T(8,128)(2,1)}, u32[]{:S(2)}) copy-start(bf16[8,160,256]{2,1,0:T(8,128)(2,1)} %table_ref) | copy-start | bytes 1966084
  8.1 6.1 %copy-start.21 = (s32[8,160]{1,0:T(8,128)S(1)}, s32[8,160]{1,0:T(8,128)}, u32[]{:S(2)}) copy-start(s32[8,160]{1,0:T(8,128)} %param.21) | copy-start | bytes 15364
  8.1 6.2 %copy-start.22 = (s32[160]{0:T(256)S(1)}, s32[160]{0:T(256)}, u32[]{:S(2)}) copy-start(s32[160]{0:T(256)} %param.22) | copy-start | bytes 1924
  8.1 19.7 %all-to-all-start = ((bf16[16,5,40,128]{3,2,1,0:T(8,128)(2,1)}), bf16[16,5,40,128]{3,2,1,0:T(8,128)(2,1)S(1)}, u32[]{:S(2)}, u32[]{:S(2)}) async-start(bf16[16,5,40,128]{3,2,1,0:T(8,128)(2,1)} %bitcast.42), calls=%async_computation | async-start | bytes 1638400 | tf_op jit(solution)/shard_map/all_to_all | solution.py:462
  27.8 47.6 %all-to-all-start.1 = ((bf16[8,2,496,128]{3,2,1,0:T(8,128)(2,1)}), bf16[8,2,496,128]{3,2,1,0:T(8,128)(2,1)S(1)}, u32[]{:S(2)}, u32[]{:S(2)}) async-start(bf16[8,2,496,128]{3,2,1,0:T(8,128)(2,1)} %pack_heads.1), calls=%async_computation.1 | async-start | bytes 4063232 | tf_op jit(solution)/shard_map/all_to_all | solution.py:477
  31.4 22.3 %collective-permute-start = (bf16[16,5,40,128]{3,2,1,0:T(8,128)(2,1)S(1)}, bf16[16,5,40,128]{3,2,1,0:T(8,128)(2,1)S(1)}, u32[]{:S(2)}, u32[]{:S(2)}) collective-permute-start(bf16[16,5,40,128]{3,2,1,0:T(8,128)(2,1)S(1)} %all-to-all-done.rest_0_), channel_id=1, source_target_pairs={{0,16},{16,32},{32,48},{48,0},{64,80},{80,96},{96,112},{112,64},{1... | collective-permute-start | bytes 2457608 | tf_op jit(solution)/shard_map/ppermute | solution.py:482
  33.4 21.2 %collective-permute-start.1 = (bf16[16,5,40,128]{3,2,1,0:T(8,128)(2,1)S(1)}, bf16[16,5,40,128]{3,2,1,0:T(8,128)(2,1)S(1)}, u32[]{:S(2)}, u32[]{:S(2)}) collective-permute-start(bf16[16,5,40,128]{3,2,1,0:T(8,128)(2,1)S(1)} %all-to-all-done.rest_0_), channel_id=1, source_target_pairs={{0,48},{16,0},{32,16},{48,32},{64,112},{80,64},{96,80},{112,96},{1... | collective-permute-start | bytes 2457608 | tf_op jit(solution)/shard_map/ppermute | solution.py:482
  35.6 38.9 %collective-permute-start.2 = (bf16[16,5,40,128]{3,2,1,0:T(8,128)(2,1)S(1)}, bf16[16,5,40,128]{3,2,1,0:T(8,128)(2,1)S(1)}, u32[]{:S(2)}, u32[]{:S(2)}) collective-permute-start(bf16[16,5,40,128]{3,2,1,0:T(8,128)(2,1)S(1)} %all-to-all-done.rest_0_), channel_id=1, source_target_pairs={{0,64},{16,80},{32,96},{48,112},{64,0},{80,16},{96,32},{112,48},{1... | collective-permute-start | bytes 2457608 | tf_op jit(solution)/shard_map/ppermute | solution.py:487
  53.7 21.7 %collective-permute-start.3 = (bf16[16,5,40,128]{3,2,1,0:T(8,128)(2,1)S(1)}, bf16[16,5,40,128]{3,2,1,0:T(8,128)(2,1)}, u32[]{:S(2)}, u32[]{:S(2)}) collective-permute-start(bf16[16,5,40,128]{3,2,1,0:T(8,128)(2,1)S(1)} %collective-permute-done.rest_1_), channel_id=1, source_target_pairs={{0,16},{16,32},{32,48},{48,0},{64,80},{80,96},{96,112},{112,64},{1... | collective-permute-start | bytes 2457608 | tf_op jit(solution)/shard_map/ppermute | solution.py:482
  74.5 0.9 copy-start.12
  75.4 10.4 %collective-permute-start.4 = (bf16[8,2,496,128]{3,2,1,0:T(8,128)(2,1)S(1)}, bf16[8,2,496,128]{3,2,1,0:T(8,128)(2,1)}, u32[]{:S(2)}, u32[]{:S(2)}) collective-permute-start(bf16[8,2,496,128]{3,2,1,0:T(8,128)(2,1)S(1)} %all-to-all-done.1.own_ref), channel_id=1, source_target_pairs={{0,1},{1,0},{2,3},{3,2},{4,5},{5,4},{6,7},{7,6},{8,9},{9,8},{10,11... | collective-permute-start | bytes 6094856 | tf_op jit(solution)/shard_map/ppermute | solution.py:492
  75.4 36.4 %collective-permute-start.5 = (bf16[16,5,40,128]{3,2,1,0:T(8,128)(2,1)}, bf16[16,5,40,128]{3,2,1,0:T(8,128)(2,1)}, u32[]{:S(2)}, u32[]{:S(2)}) collective-permute-start(bf16[16,5,40,128]{3,2,1,0:T(8,128)(2,1)} %copy-done.12), channel_id=1, source_target_pairs={{0,16},{16,32},{32,48},{48,0},{64,80},{80,96},{96,112},{112,64},{1... | collective-permute-start | bytes 2457608 | tf_op jit(solution)/shard_map/ppermute | solution.py:482
  77.4 34.4 %collective-permute-start.6 = (bf16[16,5,40,128]{3,2,1,0:T(8,128)(2,1)}, bf16[16,5,40,128]{3,2,1,0:T(8,128)(2,1)}, u32[]{:S(2)}, u32[]{:S(2)}) collective-permute-start(bf16[16,5,40,128]{3,2,1,0:T(8,128)(2,1)} %copy-done.12), channel_id=1, source_target_pairs={{0,48},{16,0},{32,16},{48,32},{64,112},{80,64},{96,80},{112,96},{1... | collective-permute-start | bytes 2457608 | tf_op jit(solution)/shard_map/ppermute | solution.py:482
  79.6 32.2 %collective-permute-start.7 = (bf16[16,5,40,128]{3,2,1,0:T(8,128)(2,1)}, bf16[16,5,40,128]{3,2,1,0:T(8,128)(2,1)}, u32[]{:S(2)}, u32[]{:S(2)}) collective-permute-start(bf16[16,5,40,128]{3,2,1,0:T(8,128)(2,1)} %collective-permute-done.3.rest_3_), channel_id=1, source_target_pairs={{0,64},{16,80},{32,96},{48,112},{64,0},{80,16},{96,32},{112,48},{1... | collective-permute-start | bytes 2457608 | tf_op jit(solution)/shard_map/ppermute | solution.py:487
  80.5 31.3 %all-to-all-start.2 = ((bf16[8,21,8,256]{3,2,1,0:T(8,128)(2,1)}), bf16[8,21,8,256]{3,2,1,0:T(8,128)(2,1)S(1)}, u32[]{:S(2)}, u32[]{:S(2)}) async-start(bf16[8,21,8,256]{3,2,1,0:T(8,128)(2,1)} %pad_maximum_fusion), calls=%async_computation.2 | async-start | bytes 1376256 | tf_op jit(solution)/shard_map/all_to_all | solution.py:497
  85.8 1.1 copy-start.15
  86.9 1.1 copy-start.17
  111.7 51.6 %copy-start = (bf16[256,1024]{1,0:T(8,128)(2,1)S(1)}, bf16[256,1024]{1,0:T(8,128)(2,1)}, u32[]{:S(2)}) copy-start(bf16[256,1024]{1,0:T(8,128)(2,1)} %col_weight_ref.1) | copy-start | bytes 1572868
  111.7 51.6 %copy-start.3 = (bf16[256,256]{1,0:T(8,128)(2,1)S(1)}, bf16[256,256]{1,0:T(8,128)(2,1)}, u32[]{:S(2)}) copy-start(bf16[256,256]{1,0:T(8,128)(2,1)} %row_out_ref.1) | copy-start | bytes 393220
  111.7 51.6 %copy-start.4 = (bf16[256,256]{1,0:T(8,128)(2,1)S(1)}, bf16[256,256]{1,0:T(8,128)(2,1)}, u32[]{:S(2)}) copy-start(bf16[256,256]{1,0:T(8,128)(2,1)} %col_out_ref.1) | copy-start | bytes 393220
  111.7 51.6 %copy-start.5 = (f32[256]{0:T(256)S(1)}, f32[256]{0:T(256)}, u32[]{:S(2)}) copy-start(f32[256]{0:T(256)} %param.23) | copy-start | bytes 3076
  111.7 51.6 %copy-start.6 = (f32[256]{0:T(256)S(1)}, f32[256]{0:T(256)}, u32[]{:S(2)}) copy-start(f32[256]{0:T(256)} %param.25) | copy-start | bytes 3076
  111.7 51.6 %copy-start.7 = (f32[256]{0:T(256)S(1)}, f32[256]{0:T(256)}, u32[]{:S(2)}) copy-start(f32[256]{0:T(256)} %param.27) | copy-start | bytes 3076
  111.7 51.6 %copy-start.8 = (f32[256]{0:T(256)S(1)}, f32[256]{0:T(256)}, u32[]{:S(2)}) copy-start(f32[256]{0:T(256)} %param.30) | copy-start | bytes 3076
  111.8 51.6 %copy-start.9 = (f32[256]{0:T(256)S(1)}, f32[256]{0:T(256)}, u32[]{:S(2)}) copy-start(f32[256]{0:T(256)} %param.32) | copy-start | bytes 3076
  111.8 51.6 %copy-start.10 = (f32[256]{0:T(256)S(1)}, f32[256]{0:T(256)}, u32[]{:S(2)}) copy-start(f32[256]{0:T(256)} %param.34) | copy-start | bytes 3076
  111.8 51.6 %copy-start.11 = (f32[256]{0:T(256)S(1)}, f32[256]{0:T(256)}, u32[]{:S(2)}) copy-start(f32[256]{0:T(256)} %param.35) | copy-start | bytes 3076
  111.8 1.2 copy-start.13
  113.0 1.0 copy-start.19
  138.5 24.8 %all-to-all-start.3 = ((bf16[64,40,128]{2,1,0:T(8,128)(2,1)}), bf16[64,40,128]{2,1,0:T(8,128)(2,1)S(1)}, u32[]{:S(2)}, u32[]{:S(2)}) async-start(bf16[64,40,128]{2,1,0:T(8,128)(2,1)} %bitcast.12), calls=%async_computation.3 | async-start | bytes 1310720 | tf_op jit(solution)/shard_map/all_to_all | solution.py:501
  163.4 1.0 copy-start.1
  164.4 1.0 copy-start.2
  (3 other events, 2.5 us)
